TPU v7x, 32 devices: a whole 2x2x4 slice. The times are simulated.
32 devices in a mesh: row: 4 (over y, x), col: 8 (over z, core).
Axes of the slice: x: 2, y: 2, z: 4, core: 2. Of those that a mesh axis runs over, the one named last changes fastest.
Arguments:
- tokens: bfloat16 [1024, 1152], P('row', 'col'), may hold values from -6 to 6
- cond: bfloat16 [4, 1152], P('row', 'col'), may hold values from -6 to 6
- w_mod: bfloat16 [2, 1152, 6, 1152], P(None, 'row', None, 'col'), may hold values from -0.1875 to 0.1875
- b_mod: float32 [2, 6, 1152], P(None, None, 'col'), may hold values from -1.8 to 1.8
- query_key_value_weight: bfloat16 [2, 1152, 3, 1152], P(None, 'row', None, 'col'), may hold values from -0.1875 to 0.1875
- b_qv: float32 [2, 2, 1152], P(None, None, 'col'), may hold values from -1.8 to 1.8
- attention_output_weight: bfloat16 [2, 1152, 1152], P(None, 'row', 'col'), may hold values from -0.75 to 0.75
- attention_output_bias: float32 [2, 1152], P(None, 'col'), may hold values from -1.8 to 1.8
- first_linear_weight: bfloat16 [2, 1152, 4608], P(None, 'row', 'col'), may hold values from -0.35355339 to 0.35355339
- first_linear_bias: float32 [2, 4608], P(None, 'col'), may hold values from -1.8 to 1.8
- second_linear_weight: bfloat16 [2, 4608, 1152], P(None, 'row', 'col'), may hold values from -0.09375 to 0.09375
- second_linear_bias: float32 [2, 1152], P(None, 'col'), may hold values from -1.8 to 1.8
- cotangent: bfloat16 [1024, 1152], P('row', 'col'), may hold values from -6 to 6
Outputs:
- output: bfloat16 [1024, 1152], P('row', 'col')
- grad_tokens: float32 [1024, 1152], P('row', 'col')
- grad_cond: float32 [4, 1152], P('row', 'col')
- grad_w_mod: float32 [2, 1152, 6, 1152], P(None, 'row', None, 'col')
- grad_b_mod: float32 [2, 6, 1152], P(None, None, 'col')
- grad_w_qkv: float32 [2, 1152, 3, 1152], P(None, 'row', None, 'col')
- grad_b_qv: float32 [2, 2, 1152], P(None, None, 'col')
- grad_w_out: float32 [2, 1152, 1152], P(None, 'row', 'col')
- grad_b_out: float32 [2, 1152], P(None, 'col')
- grad_w_fc1: float32 [2, 1152, 4608], P(None, 'row', 'col')
- grad_b_fc1: float32 [2, 4608], P(None, 'col')
- grad_w_fc2: float32 [2, 4608, 1152], P(None, 'row', 'col')
- grad_b_fc2: float32 [2, 1152], P(None, 'col')
All inputs are finite; a program needn't handle non-finite values.
Results may differ from a plain program's by a relative error of at most 0.023.
The roundings to bfloat16 on the way count: a program that leaves them out, or rounds other values in their place, can miss the bound.
Values may be sent and summed in bfloat16 or wider, within the bound.
A program may use at most 128 MiB of HBM per device.

v0:
```python
import jax
import jax.numpy as jnp
from jax import lax
from jax.sharding import PartitionSpec as P

D = 1152
HEAD = 72
LAYERS = 2


EPS = 1e-06


def gelu_tanh(values):
    return jax.nn.gelu(values, approximate=True)


def seq_sum(values, seq_count):
    return jnp.sum(values.reshape(seq_count, -1, values.shape[-1]), axis=1)


def modulate(normed, offset, stretch):
    seq_count = offset.shape[0]
    shaped = normed.reshape(seq_count, -1, offset.shape[1])
    return (shaped * (1.0 + stretch[:, None]) + offset[:, None]).reshape(normed.shape)


def gated(values, factor):
    seq_count = factor.shape[0]
    return (values.reshape(seq_count, -1, factor.shape[1]) * factor[:, None]).reshape(values.shape)


def gather_features(pieces):
    return lax.all_gather(pieces, "col", axis=1, tiled=True)


def forward_product(gathered, weight):
    return jnp.dot(
        gathered,
        lax.all_gather(weight, "row", axis=0, tiled=True),
        preferred_element_type=jnp.float32,
    )


def scattered_grad(grad_rows, weight):
    partials = lax.dot_general(
        grad_rows,
        lax.all_gather(weight, "row", axis=0, tiled=True),
        (((1,), (1,)), ((), ())),
        preferred_element_type=jnp.float32,
    )
    return lax.psum_scatter(partials, "col", scatter_dimension=1, tiled=True)


def input_grad(grad_rows, weight):
    result = scattered_grad(grad_rows, weight)
    return result


def weight_grad(gathered, grad_rows):
    return lax.psum_scatter(
        lax.dot_general(
            gathered, grad_rows, (((0,), (0,)), ((), ())), preferred_element_type=jnp.float32
        ),
        "row",
        scatter_dimension=0,
        tiled=True,
    )


def normalize(stream):
    average = lax.psum(jnp.sum(stream, 1, keepdims=True), "col") / D
    centred = stream - average
    spread = lax.psum(jnp.sum(centred * centred, 1, keepdims=True), "col") / D
    inverse = lax.rsqrt(spread + EPS)
    return (centred * inverse, inverse)


def normalize_back(grad_normed, normed, inverse):
    grad_sum, cross_sum = lax.psum(
        (jnp.sum(grad_normed, 1, keepdims=True), jnp.sum(grad_normed * normed, 1, keepdims=True)),
        "col",
    )
    return inverse * (grad_normed - grad_sum / D - normed * (cross_sum / D))


def attend(query_rows, key_rows, value_rows, score_scale):
    scores = (
        jnp.einsum("sqhe,skhe->shqk", query_rows, key_rows, preferred_element_type=jnp.float32)
        * score_scale
    )
    highest = jnp.max(scores, axis=-1, keepdims=True)
    expd = jnp.exp(scores - highest)
    summed = jnp.sum(expd, axis=-1, keepdims=True)
    probs = (expd / summed).astype(jnp.bfloat16)
    attended_values = jnp.einsum(
        "shqk,skhe->sqhe", probs, value_rows, preferred_element_type=jnp.float32
    )
    return (attended_values.astype(jnp.bfloat16), highest + jnp.log(summed))


def attend_back(query_rows, key_rows, value_rows, log_total, grad_attended, score_scale):
    scores = (
        jnp.einsum("sqhe,skhe->shqk", query_rows, key_rows, preferred_element_type=jnp.float32)
        * score_scale
    )
    weights = jnp.exp(scores - log_total)
    grad_weights = jnp.einsum(
        "sqhe,skhe->shqk", grad_attended, value_rows, preferred_element_type=jnp.float32
    )
    grad_value = jnp.einsum(
        "shqk,sqhe->skhe",
        weights.astype(jnp.bfloat16),
        grad_attended,
        preferred_element_type=jnp.float32,
    )
    grad_scores = (
        weights * (grad_weights - jnp.sum(weights * grad_weights, axis=-1, keepdims=True))
    ).astype(jnp.bfloat16)
    grad_query = (
        jnp.einsum("shqk,skhe->sqhe", grad_scores, key_rows, preferred_element_type=jnp.float32)
        * score_scale
    )
    grad_key = (
        jnp.einsum("shqk,sqhe->skhe", grad_scores, query_rows, preferred_element_type=jnp.float32)
        * score_scale
    )
    return (
        grad_query.astype(jnp.bfloat16),
        grad_key.astype(jnp.bfloat16),
        grad_value.astype(jnp.bfloat16),
    )


def per_device(
    tokens,
    cond,
    w_mod,
    b_mod,
    query_key_value_weight,
    b_qv,
    attention_output_weight,
    attention_output_bias,
    first_linear_weight,
    first_linear_bias,
    second_linear_weight,
    second_linear_bias,
    cotangent,
):
    seq_count = cond.shape[0]
    row_total = tokens.shape[0]
    local_width = tokens.shape[1]
    heads_shape = (seq_count, row_total // seq_count, local_width // HEAD, HEAD)
    score_scale = HEAD ** (-0.5)
    cond_float = cond.astype(jnp.float32)
    signal = jax.nn.silu(cond_float).astype(jnp.bfloat16)
    signal_full = gather_features(signal)
    stream = tokens.astype(jnp.float32)
    saved = []
    for layer_index in range(LAYERS):
        modulation = (
            forward_product(signal_full, w_mod[layer_index].reshape(w_mod.shape[1], -1)).reshape(
                seq_count, 6, local_width
            )
            + b_mod[layer_index]
        )
        normed1, inverse1 = normalize(stream)
        hidden_first = modulate(normed1, modulation[:, 0], modulation[:, 1]).astype(jnp.bfloat16)
        hidden1_full = gather_features(hidden_first)
        query_key_value_bias = jnp.stack(
            [b_qv[layer_index, 0], jnp.zeros_like(b_qv[layer_index, 0]), b_qv[layer_index, 1]]
        )
        query_key_value = forward_product(
            hidden1_full,
            query_key_value_weight[layer_index].reshape(query_key_value_weight.shape[1], -1),
        ).reshape(row_total, 3, local_width)
        query_key_value = (query_key_value + query_key_value_bias).astype(jnp.bfloat16)
        query_rows = query_key_value[:, 0].reshape(heads_shape)
        key_rows = query_key_value[:, 1].reshape(heads_shape)
        value_rows = query_key_value[:, 2].reshape(heads_shape)
        attended_values, log_total = attend(query_rows, key_rows, value_rows, score_scale)
        attended_values = attended_values.reshape(row_total, local_width)
        attended_full = gather_features(attended_values)
        attention_branch = (
            forward_product(attended_full, attention_output_weight[layer_index])
            + attention_output_bias[layer_index]
        )
        stream = stream + gated(attention_branch, modulation[:, 2])
        normed2, inverse2 = normalize(stream)
        hidden_second = modulate(normed2, modulation[:, 3], modulation[:, 4]).astype(jnp.bfloat16)
        hidden2_full = gather_features(hidden_second)
        preactivation_values = (
            forward_product(hidden2_full, first_linear_weight[layer_index])
            + first_linear_bias[layer_index]
        )
        activated_hidden = gelu_tanh(preactivation_values).astype(jnp.bfloat16)
        activated_full = gather_features(activated_hidden)
        feedforward_branch = (
            forward_product(activated_full, second_linear_weight[layer_index])
            + second_linear_bias[layer_index]
        )
        stream = stream + gated(feedforward_branch, modulation[:, 5])
        kept = (hidden_first, attended_values, hidden_second, activated_hidden)
        saved.append(
            (
                modulation,
                normed1,
                inverse1,
                query_rows,
                key_rows,
                value_rows,
                log_total,
                attention_branch,
                normed2,
                inverse2,
                preactivation_values,
                feedforward_branch,
                kept,
            )
        )
    output = stream.astype(jnp.bfloat16)
    grad_stream = cotangent.astype(jnp.float32)
    grad_signal = jnp.zeros((seq_count, local_width), jnp.float32)
    results = {}
    for layer_index in reversed(range(LAYERS)):
        (
            modulation,
            normed1,
            inverse1,
            query_rows,
            key_rows,
            value_rows,
            log_total,
            attention_branch,
            normed2,
            inverse2,
            preactivation_values,
            feedforward_branch,
            kept,
        ) = saved[layer_index]
        hidden1_full, attended_full, hidden2_full, activated_full = (
            lax.all_gather(kept[0], "col", axis=1, tiled=True),
            lax.all_gather(kept[1], "col", axis=1, tiled=True),
            lax.all_gather(kept[2], "col", axis=1, tiled=True),
            lax.all_gather(kept[3], "col", axis=1, tiled=True),
        )
        grad_gate2 = seq_sum(grad_stream * feedforward_branch, seq_count)
        grad_branch2 = gated(grad_stream, modulation[:, 5]).astype(jnp.bfloat16)
        grad_fc2 = weight_grad(activated_full, grad_branch2)
        bias_fc2 = jnp.sum(grad_branch2.astype(jnp.float32), 0)
        grad_activated = input_grad(grad_branch2, second_linear_weight[layer_index])
        grad_pre = jax.vjp(gelu_tanh, preactivation_values)[1](grad_activated)[0].astype(
            jnp.bfloat16
        )
        grad_fc1 = weight_grad(hidden2_full, grad_pre)
        bias_fc1 = jnp.sum(grad_pre.astype(jnp.float32), 0)
        grad_hidden2 = input_grad(grad_pre, first_linear_weight[layer_index])
        grad_shift2 = seq_sum(grad_hidden2, seq_count)
        grad_scale2 = seq_sum(grad_hidden2 * normed2, seq_count)
        grad_stream = grad_stream + normalize_back(
            gated(grad_hidden2, 1.0 + modulation[:, 4]), normed2, inverse2
        )
        grad_gate1 = seq_sum(grad_stream * attention_branch, seq_count)
        grad_branch1 = gated(grad_stream, modulation[:, 2]).astype(jnp.bfloat16)
        grad_out_w = weight_grad(attended_full, grad_branch1)
        bias_out = jnp.sum(grad_branch1.astype(jnp.float32), 0)
        grad_attended = (
            input_grad(grad_branch1, attention_output_weight[layer_index])
            .astype(jnp.bfloat16)
            .reshape(heads_shape)
        )
        grad_query, grad_key, grad_value = attend_back(
            query_rows, key_rows, value_rows, log_total, grad_attended, score_scale
        )
        grad_qkv = jnp.stack(
            [
                grad_query.reshape(row_total, local_width),
                grad_key.reshape(row_total, local_width),
                grad_value.reshape(row_total, local_width),
            ],
            axis=1,
        )
        grad_qkv_flat = grad_qkv.reshape(row_total, -1)
        grad_qkv_w = weight_grad(hidden1_full, grad_qkv_flat).reshape(-1, 3, local_width)
        qkv_sums = jnp.sum(grad_qkv.astype(jnp.float32), 0)
        bias_qv = jnp.stack([qkv_sums[0], qkv_sums[2]])
        grad_hidden1 = input_grad(
            grad_qkv_flat,
            query_key_value_weight[layer_index].reshape(query_key_value_weight.shape[1], -1),
        )
        grad_shift1 = seq_sum(grad_hidden1, seq_count)
        grad_scale1 = seq_sum(grad_hidden1 * normed1, seq_count)
        grad_stream = grad_stream + normalize_back(
            gated(grad_hidden1, 1.0 + modulation[:, 1]), normed1, inverse1
        )
        grad_mod = jnp.stack(
            [grad_shift1, grad_scale1, grad_gate1, grad_shift2, grad_scale2, grad_gate2], axis=1
        ).astype(jnp.bfloat16)
        grad_mod_flat = grad_mod.reshape(seq_count, -1)
        grad_mod_w = weight_grad(signal_full, grad_mod_flat).reshape(-1, 6, local_width)
        bias_mod = jnp.sum(grad_mod.astype(jnp.float32), 0)
        grad_signal = grad_signal + input_grad(
            grad_mod_flat, w_mod[layer_index].reshape(w_mod.shape[1], -1)
        )
        bias_sums = lax.psum((bias_mod, bias_qv, bias_out, bias_fc1, bias_fc2), "row")
        results[layer_index] = (
            grad_mod_w,
            bias_sums[0],
            grad_qkv_w,
            bias_sums[1],
            grad_out_w,
            bias_sums[2],
            grad_fc1,
            bias_sums[3],
            grad_fc2,
            bias_sums[4],
        )
    grad_cond = jax.vjp(jax.nn.silu, cond_float)[1](grad_signal)[0]
    stacked = [
        jnp.stack([results[layer_index][member] for layer_index in range(LAYERS)])
        for member in range(10)
    ]
    return (
        output,
        grad_stream,
        grad_cond,
        stacked[0],
        stacked[1],
        stacked[2],
        stacked[3],
        stacked[4],
        stacked[5],
        stacked[6],
        stacked[7],
        stacked[8],
        stacked[9],
    )


def solution(mesh):
    in_specs = (
        P("row", "col"),
        P("row", "col"),
        P(None, "row", None, "col"),
        P(None, None, "col"),
        P(None, "row", None, "col"),
        P(None, None, "col"),
        P(None, "row", "col"),
        P(None, "col"),
        P(None, "row", "col"),
        P(None, "col"),
        P(None, "row", "col"),
        P(None, "col"),
        P("row", "col"),
    )
    out_specs = (
        P("row", "col"),
        P("row", "col"),
        P("row", "col"),
        P(None, "row", None, "col"),
        P(None, None, "col"),
        P(None, "row", None, "col"),
        P(None, None, "col"),
        P(None, "row", "col"),
        P(None, "col"),
        P(None, "row", "col"),
        P(None, "col"),
        P(None, "row", "col"),
        P(None, "col"),
    )
    return jax.shard_map(
        per_device, mesh=mesh, in_specs=in_specs, out_specs=out_specs, check_vma=False
    )
```

profile of v0, /device:TPU:0, one launch (start us, length us, event | category | flops | bytes accessed | tf_op | source)
XLA Modules:
  0.0 1168.2 jit_solution(13181938890689784427)
XLA Ops:
  15.7 18.1 %all-reduce = bf16[1152]{0:T(1024)(128)(2,1)S(1)} all-reduce(bf16[1152]{0:T(1024)(128)(2,1)S(1)} %dynamic-update-slice), channel_id=1, replica_groups=mesh['row'=4,'col'=8] {'col'}, use_global_device_ids=true, to_apply=%add | all-reduce | flops 1152 | bytes 4608 | tf_op jit(solution)/shard_map/reshape
  62.7 15.7 %all_gather.78 = bf16[1152,432]{1,0:T(8,128)(2,1)S(1)} all-gather(bf16[288,432]{1,0:T(8,128)(2,1)S(1)} %copy.71), channel_id=1, replica_groups=mesh['row'=4,'col'=8] {'row'}, dimensions={0}, use_global_device_ids=true | all-gather | bytes 1244160 | tf_op jit(solution)/shard_map/all_gather | solution.py:40
  78.7 19.5 %all-gather = bf16[1,1152,144]{2,0,1:T(2,128)(2,1)S(1)} all-gather(bf16[1,288,144]{2,0,1:T(2,128)(2,1)S(1)} %copy.111), channel_id=2, replica_groups=mesh['row'=4,'col'=8] {'row'}, dimensions={1}, use_global_device_ids=true | all-gather | bytes 414720 | tf_op jit(solution)/shard_map/all_gather | solution.py:40
  109.4 15.4 %all_gather.77 = bf16[256,1152]{0,1:T(8,128)(2,1)S(1)} all-gather(bf16[256,144]{0,1:T(8,128)(2,1)S(1)} %fusion.67), channel_id=1, replica_groups=mesh['row'=4,'col'=8] {'col'}, dimensions={1}, use_global_device_ids=true | all-gather | bytes 663552 | tf_op jit(solution)/shard_map/all_gather | solution.py:34
  126.4 15.1 %all_gather.79 = bf16[256,1152]{0,1:T(8,128)(2,1)S(1)} all-gather(bf16[256,144]{0,1:T(8,128)(2,1)S(1)} %bitcast.322), channel_id=1, replica_groups=mesh['row'=4,'col'=8] {'col'}, dimensions={1}, use_global_device_ids=true | all-gather | bytes 663552 | tf_op jit(solution)/shard_map/all_gather | solution.py:34
  142.5 17.5 %psum.184 = f32[256,1]{0,1:T(1,128)S(1)} all-reduce(f32[256,1]{0,1:T(1,128)S(1)} %bitcast.417), channel_id=1, replica_groups=mesh['row'=4,'col'=8] {'col'}, use_global_device_ids=true, to_apply=%region_7.8 | all-reduce | flops 256 | bytes 2048 | tf_op jit(solution)/shard_map/psum | solution.py:72
  173.7 15.1 %all_gather.81 = bf16[256,1152]{0,1:T(8,128)(2,1)S(1)} all-gather(bf16[256,144]{0,1:T(8,128)(2,1)S(1)} %add_convert_fusion.5), channel_id=1, replica_groups=mesh['row'=4,'col'=8] {'col'}, dimensions={1}, use_global_device_ids=true | all-gather | bytes 663552 | tf_op jit(solution)/shard_map/all_gather | solution.py:34
  200.3 15.8 %all-gather.3 = bf16[1,1152,144]{2,0,1:T(2,128)(2,1)S(1)} all-gather(bf16[1,288,144]{2,0,1:T(2,128)(2,1)} %copy.113), channel_id=5, replica_groups=mesh['row'=4,'col'=8] {'row'}, dimensions={1}, use_global_device_ids=true | all-gather | bytes 414720 | tf_op jit(solution)/shard_map/all_gather | solution.py:40
  262.8 17.7 %all_gather.86 = bf16[256,1152]{0,1:T(8,128)(2,1)S(1)} all-gather(bf16[256,144]{0,1:T(8,128)(2,1)S(1)} %add_convert_fusion.4), channel_id=1, replica_groups=mesh['row'=4,'col'=8] {'col'}, dimensions={1}, use_global_device_ids=true | all-gather | bytes 663552 | tf_op jit(solution)/shard_map/all_gather | solution.py:34
  283.0 17.8 %all_gather.88 = bf16[256,1152]{0,1:T(8,128)(2,1)S(1)} all-gather(bf16[256,144]{0,1:T(8,128)(2,1)S(1)} %bitcast.323), channel_id=1, replica_groups=mesh['row'=4,'col'=8] {'col'}, dimensions={1}, use_global_device_ids=true | all-gather | bytes 663552 | tf_op jit(solution)/shard_map/all_gather | solution.py:34
  302.3 16.4 %psum.188 = f32[256,1]{0,1:T(1,128)} all-reduce(f32[256,1]{0,1:T(1,128)} %bitcast.405), channel_id=1, replica_groups=mesh['row'=4,'col'=8] {'col'}, use_global_device_ids=true, to_apply=%region_17.18 | all-reduce | flops 256 | bytes 2048 | tf_op jit(solution)/shard_map/psum | solution.py:72
  321.5 14.3 %psum.189 = f32[256,1]{0,1:T(1,128)} all-reduce(f32[256,1]{0,1:T(1,128)} %bitcast.410), channel_id=1, replica_groups=mesh['row'=4,'col'=8] {'col'}, use_global_device_ids=true, to_apply=%region_19.20 | all-reduce | flops 256 | bytes 2048 | tf_op jit(solution)/shard_map/psum | solution.py:74
  338.0 15.9 %all_gather.90 = bf16[256,1152]{0,1:T(8,128)(2,1)} all-gather(bf16[256,144]{0,1:T(8,128)(2,1)S(1)} %add_convert_fusion.3), channel_id=1, replica_groups=mesh['row'=4,'col'=8] {'col'}, dimensions={1}, use_global_device_ids=true | all-gather | bytes 663552 | tf_op jit(solution)/shard_map/all_gather | solution.py:34
  361.2 29.5 %reduce-scatter.32.cloned.1.call-done = f32[256,144]{0,1:T(8,128)} async-done(((f32[256,1152]{0,1:T(8,128)}), f32[256,144]{0,1:T(8,128)}) %reduce-scatter.32.cloned.1.call-update) | async-done | bytes 147472 | tf_op jit(solution)/shard_map/reduce_scatter | solution.py:52
  392.5 15.0 %all-reduce.4 = (f32[256,1]{0,1:T(1,128)}, f32[256,1]{0,1:T(1,128)}) all-reduce(f32[256,1]{0,1:T(1,128)} %bitcast.397, f32[256,1]{0,1:T(1,128)} %bitcast.398), channel_id=1, replica_groups=mesh['row'=4,'col'=8] {'col'}, use_global_device_ids=true, to_apply=%region_25.26 | all-reduce | flops 512 | bytes 4096 | tf_op jit(solution)/shard_map/psum | solution.py:80
  430.3 30.8 %reduce-scatter.34.cloned.1.call-done = f32[256,144]{0,1:T(8,128)} async-done(((f32[256,1152]{0,1:T(8,128)}), f32[256,144]{0,1:T(8,128)}) %reduce-scatter.34.cloned.1.call-update) | async-done | bytes 147472 | tf_op jit(solution)/shard_map/reduce_scatter | solution.py:52
  467.1 31.1 %reduce-scatter.36.cloned.1.call-done = f32[256,144]{0,1:T(8,128)} async-done(((f32[256,1152]{0,1:T(8,128)}), f32[256,144]{0,1:T(8,128)}) %reduce-scatter.36.cloned.1.call-update) | async-done | bytes 147472 | tf_op jit(solution)/shard_map/reduce_scatter | solution.py:52
  499.8 13.9 %all-reduce.3 = (f32[256,1]{0,1:T(1,128)S(1)}, f32[256,1]{0,1:T(1,128)S(1)}) all-reduce(f32[256,1]{0,1:T(1,128)S(1)} %bitcast.399, f32[256,1]{0,1:T(1,128)S(1)} %bitcast.400), channel_id=1, replica_groups=mesh['row'=4,'col'=8] {'col'}, use_global_device_ids=true, to_apply=%region_32.33 | all-reduce | flops 512 | bytes 4096 | tf_op jit(solution)/shard_map/psum | solution.py:80
  520.1 53.5 %reduce-scatter.38.cloned.1.call-done = f32[256,576]{0,1:T(8,128)} async-done(((f32[256,4608]{0,1:T(8,128)}), f32[256,576]{0,1:T(8,128)}) %reduce-scatter.38.cloned.1.call-update) | async-done | bytes 589840 | tf_op jit(solution)/shard_map/reduce_scatter | solution.py:52
  578.4 31.3 %reduce-scatter.40.cloned.1.call-done = f32[256,144]{0,1:T(8,128)} async-done(((f32[256,1152]{0,1:T(8,128)}), f32[256,144]{0,1:T(8,128)}) %reduce-scatter.40.cloned.1.call-update) | async-done | bytes 147472 | tf_op jit(solution)/shard_map/reduce_scatter | solution.py:52
  629.3 30.9 %reduce-scatter.42.cloned.1.call-done = f32[256,144]{0,1:T(8,128)} async-done(((f32[256,1152]{0,1:T(8,128)}), f32[256,144]{0,1:T(8,128)}) %reduce-scatter.42.cloned.1.call-update) | async-done | bytes 147472 | tf_op jit(solution)/shard_map/reduce_scatter | solution.py:52
  696.3 14.1 %all-reduce.1 = (f32[256,1]{0,1:T(1,128)S(1)}, f32[256,1]{0,1:T(1,128)S(1)}) all-reduce(f32[256,1]{0,1:T(1,128)S(1)} %bitcast.403, f32[256,1]{0,1:T(1,128)S(1)} %bitcast.404), channel_id=1, replica_groups=mesh['row'=4,'col'=8] {'col'}, use_global_device_ids=true, to_apply=%region_45.46 | all-reduce | flops 512 | bytes 4096 | tf_op jit(solution)/shard_map/psum | solution.py:80
  734.0 31.7 %reduce-scatter.48.cloned.1.call-done = f32[288,432]{1,0:T(8,128)} async-done(((f32[1152,432]{1,0:T(8,128)}), f32[288,432]{1,0:T(8,128)}) %reduce-scatter.48.cloned.1.call-update) | async-done | bytes 497680 | tf_op jit(solution)/shard_map/reduce_scatter | solution.py:61
  767.1 42.5 %reduce-scatter.56.cloned.1.call-done = f32[1152,144]{0,1:T(8,128)} async-done(((f32[4608,144]{0,1:T(8,128)}), f32[1152,144]{0,1:T(8,128)}) %reduce-scatter.56.cloned.1.call-update) | async-done | bytes 663568 | tf_op jit(solution)/shard_map/reduce_scatter | solution.py:61
  809.6 43.4 %reduce-scatter.54.cloned.1.call-done = f32[1152,144]{0,1:T(8,128)} async-done(((f32[4608,144]{0,1:T(8,128)}), f32[1152,144]{0,1:T(8,128)}) %reduce-scatter.54.cloned.1.call-update) | async-done | bytes 663568 | tf_op jit(solution)/shard_map/reduce_scatter | solution.py:61
  855.5 29.6 %reduce-scatter.62.cloned.1.call-done = f32[288,144]{1,0:T(8,128)} async-done(((f32[1152,144]{1,0:T(8,128)}), f32[288,144]{1,0:T(8,128)}) %reduce-scatter.62.cloned.1.call-update) | async-done | bytes 165904
  887.0 43.5 %reduce-scatter.52.cloned.1.call-done = f32[288,576]{1,0:T(8,128)} async-done(((f32[1152,576]{1,0:T(8,128)}), f32[288,576]{1,0:T(8,128)}) %reduce-scatter.52.cloned.1.call-update) | async-done | bytes 663568 | tf_op jit(solution)/shard_map/reduce_scatter | solution.py:61
  930.4 45.4 %reduce-scatter.50.cloned.1.call-done = f32[288,576]{1,0:T(8,128)} async-done(((f32[1152,576]{1,0:T(8,128)}), f32[288,576]{1,0:T(8,128)}) %reduce-scatter.50.cloned.1.call-update) | async-done | bytes 663568 | tf_op jit(solution)/shard_map/reduce_scatter | solution.py:61
  978.5 15.4 %all-reduce.5 = (f32[1,6,144]{2,1,0:T(8,128)S(1)}, f32[1,6,144]{2,1,0:T(8,128)S(1)}, f32[1,2,144]{2,1,0:T(2,128)S(1)}, f32[1,2,144]{2,1,0:T(2,128)S(1)}, f32[1,1...) all-reduce(f32[1,6,144]{2,1,0:T(8,128)S(1)} %bitcast_convert_fusion, ...), channel_id=1, replica_groups=mesh['row'=4,'col'=8] {'row'}, use_global_device_ids=true, to_apply=%region_63.64 | all-reduce | flops 4032 | bytes 32256 | tf_op jit(solution)/shard_map/psum | solution.py:305
  1010.6 37.1 %reduce-scatter.46.cloned.1.call-done = f32[288,432]{1,0:T(8,128)} async-done(((f32[1152,432]{1,0:T(8,128)}), f32[288,432]{1,0:T(8,128)}) %reduce-scatter.46.cloned.1.call-update) | async-done | bytes 497680 | tf_op jit(solution)/shard_map/reduce_scatter | solution.py:61
  1050.3 52.6 %reduce-scatter.60.cloned.1.call-done = f32[288,864]{1,0:T(8,128)} async-done(((f32[1152,864]{1,0:T(8,128)}), f32[288,864]{1,0:T(8,128)}) %reduce-scatter.60.cloned.1.call-update) | async-done | bytes 995344
  1104.5 53.5 %reduce-scatter.58.cloned.1.call-done = f32[288,864]{1,0:T(8,128)} async-done(((f32[1152,864]{1,0:T(8,128)}), f32[288,864]{1,0:T(8,128)}) %reduce-scatter.58.cloned.1.call-update) | async-done | bytes 995344
  (485 shorter events, 292.8 us)
Async XLA Ops:
  7.2 94.4 %all-gather.19.cloned.1.call-start = ((), (), s32[]{:S(2)}) async-start(), calls=%async_computation.21 | async-start | bytes 2580480 | tf_op jit(solution)/shard_map/all_gather | solution.py:40
  9.7 95.4 %all-gather.15.cloned.1.call-start = ((), (), s32[]{:S(2)}) async-start(), calls=%async_computation.19 | async-start | bytes 2580480 | tf_op jit(solution)/shard_map/all_gather | solution.py:40
  10.9 178.0 %all-gather.23.cloned.1.call-start = ((), (), s32[]{:S(2)}) async-start(), calls=%async_computation.37 | async-start | bytes 1843200 | tf_op jit(solution)/shard_map/all_gather | solution.py:40
  11.9 181.7 %all-gather.29.cloned.1.call-start = ((), (), s32[]{:S(2)}) async-start(), calls=%async_computation.40 | async-start | bytes 1658880 | tf_op jit(solution)/shard_map/all_gather | solution.py:40
  13.0 219.1 %all-gather.25.cloned.1.call-start = ((), (), s32[]{:S(2)}) async-start(), calls=%async_computation.38 | async-start | bytes 1658880 | tf_op jit(solution)/shard_map/all_gather | solution.py:40
  13.6 218.5 %all-gather.17.cloned.1.call-start = ((), (), s32[]{:S(2)}) async-start(), calls=%async_computation.20 | async-start | bytes 2654208 | tf_op jit(solution)/shard_map/all_gather | solution.py:34
  48.0 60.8 %copy-start.54 = (f32[256,1]{0,1:T(1,128)}, f32[256,1]{0,1:T(1,128)S(1)}, u32[]{:S(2)}) copy-start(f32[256,1]{0,1:T(1,128)S(1)} %broadcast_multiply_fusion.13) | copy-start | bytes 3076
  108.8 64.8 %copy-start.68 = (f32[1,1,144]{2,1,0:T(1,128)}, f32[1,1,144]{2,1,0:T(1,128)S(1)}, u32[]{:S(2)}) copy-start(f32[1,1,144]{2,1,0:T(1,128)S(1)} %get-tuple-element.152) | copy-start | bytes 1732
  108.8 123.3 %copy-start.84 = (f32[1,1,144]{2,1,0:T(1,128)}, f32[1,1,144]{2,1,0:T(1,128)S(1)}, u32[]{:S(2)}) copy-start(f32[1,1,144]{2,1,0:T(1,128)S(1)} %get-tuple-element.150) | copy-start | bytes 1732
  126.4 62.5 %copy-start.105 = (f32[576]{0:T(1024)S(1)}, f32[576]{0:T(1024)}, u32[]{:S(2)}) copy-start(f32[576]{0:T(1024)} %get-tuple-element.71) | copy-start | bytes 6916
  192.2 161.7 %all-gather.27.cloned.1.call-start = ((), (), s32[]{:S(2)}) async-start(), calls=%async_computation.39 | async-start | bytes 1843200 | tf_op jit(solution)/shard_map/all_gather | solution.py:40
  193.0 161.0 %reduce-scatter.30.cloned.1.call-start = ((), (), s32[]{:S(2)}) async-start(), calls=%async_computation.23 | async-start | bytes 5308416 | tf_op jit(solution)/shard_map/reduce_scatter | solution.py:52
  193.6 69.1 %copy-start.70 = (f32[1,1,144]{2,1,0:T(1,128)}, f32[1,1,144]{2,1,0:T(1,128)S(1)}, u32[]{:S(2)}) copy-start(f32[1,1,144]{2,1,0:T(1,128)S(1)} %get-tuple-element.149) | copy-start | bytes 1732
  198.2 192.5 %reduce-scatter.32.cloned.1.call-start = ((), (), s32[]{:S(2)}) async-start(), calls=%async_computation.24 | async-start | bytes 1327104 | tf_op jit(solution)/shard_map/reduce_scatter | solution.py:52
  360.5 62.4 %all-gather.21.cloned.1.call-start = ((), (), s32[]{:S(2)}) async-start(), calls=%async_computation.22 | async-start | bytes 2654208 | tf_op jit(solution)/shard_map/all_gather | solution.py:34
  361.1 100.0 %reduce-scatter.34.cloned.1.call-start = ((), (), s32[]{:S(2)}) async-start(), calls=%async_computation.25 | async-start | bytes 1327104 | tf_op jit(solution)/shard_map/reduce_scatter | solution.py:52
  428.9 69.2 %reduce-scatter.36.cloned.1.call-start = ((), (), s32[]{:S(2)}) async-start(), calls=%async_computation.26 | async-start | bytes 1327104 | tf_op jit(solution)/shard_map/reduce_scatter | solution.py:52
  467.0 106.5 %reduce-scatter.38.cloned.1.call-start = ((), (), s32[]{:S(2)}) async-start(), calls=%async_computation.27 | async-start | bytes 5308416 | tf_op jit(solution)/shard_map/reduce_scatter | solution.py:52
  520.0 89.7 %reduce-scatter.40.cloned.1.call-start = ((), (), s32[]{:S(2)}) async-start(), calls=%async_computation.28 | async-start | bytes 1327104 | tf_op jit(solution)/shard_map/reduce_scatter | solution.py:52
  578.3 82.0 %reduce-scatter.42.cloned.1.call-start = ((), (), s32[]{:S(2)}) async-start(), calls=%async_computation.29 | async-start | bytes 1327104 | tf_op jit(solution)/shard_map/reduce_scatter | solution.py:52
  629.0 66.2 %reduce-scatter.44.cloned.1.call-start = ((), (), s32[]{:S(2)}) async-start(), calls=%async_computation.30 | async-start | bytes 1327104 | tf_op jit(solution)/shard_map/reduce_scatter | solution.py:52
  664.2 68.5 %reduce-scatter.64.cloned.1.call-start = ((), (), s32[]{:S(2)}) async-start(), calls=%async_computation.44 | async-start | bytes 1474560
  665.7 100.1 %reduce-scatter.48.cloned.1.call-start = ((), (), s32[]{:S(2)}) async-start(), calls=%async_computation.32 | async-start | bytes 2949120 | tf_op jit(solution)/shard_map/reduce_scatter | solution.py:61
  667.7 141.9 %reduce-scatter.56.cloned.1.call-start = ((), (), s32[]{:S(2)}) async-start(), calls=%async_computation.36 | async-start | bytes 3317760 | tf_op jit(solution)/shard_map/reduce_scatter | solution.py:61
  671.8 181.1 %reduce-scatter.54.cloned.1.call-start = ((), (), s32[]{:S(2)}) async-start(), calls=%async_computation.35 | async-start | bytes 3317760 | tf_op jit(solution)/shard_map/reduce_scatter | solution.py:61
  675.9 209.1 %reduce-scatter.62.cloned.1.call-start = ((), (), s32[]{:S(2)}) async-start(), calls=%async_computation.43 | async-start | bytes 1474560
  678.3 252.1 %reduce-scatter.52.cloned.1.call-start = ((), (), s32[]{:S(2)}) async-start(), calls=%async_computation.34 | async-start | bytes 3686400 | tf_op jit(solution)/shard_map/reduce_scatter | solution.py:61
  680.7 295.2 %reduce-scatter.50.cloned.1.call-start = ((), (), s32[]{:S(2)}) async-start(), calls=%async_computation.33 | async-start | bytes 3686400 | tf_op jit(solution)/shard_map/reduce_scatter | solution.py:61
  684.1 325.0 %reduce-scatter.66.cloned.1.call-start = ((), (), s32[]{:S(2)}) async-start(), calls=%async_computation.45 | async-start | bytes 663552
  714.1 333.7 %reduce-scatter.46.cloned.1.call-start = ((), (), s32[]{:S(2)}) async-start(), calls=%async_computation.31 | async-start | bytes 2949120 | tf_op jit(solution)/shard_map/reduce_scatter | solution.py:61
  716.1 386.8 %reduce-scatter.60.cloned.1.call-start = ((), (), s32[]{:S(2)}) async-start(), calls=%async_computation.42 | async-start | bytes 5160960
  726.4 431.6 %reduce-scatter.58.cloned.1.call-start = ((), (), s32[]{:S(2)}) async-start(), calls=%async_computation.41 | async-start | bytes 5160960
  (109 other events, 1547.2 us)
Sparse Core Ops, SparseCore 0:
  10.4 37.7 all-gather.18
  50.6 43.8 all-gather.14
  96.9 31.3 all-gather.22
  130.0 28.9 all-gather.28
  160.7 28.9 all-gather.24
  192.3 31.0 all-gather.16
  225.8 29.2 all-gather.26
  257.4 64.7 reduce-scatter.29
  360.6 29.9 reduce-scatter.31
  392.7 30.1 all-gather.20
  429.1 31.9 reduce-scatter.33
  467.1 30.9 reduce-scatter.35
  520.1 53.3 reduce-scatter.37
  578.4 31.1 reduce-scatter.39
  629.1 31.0 reduce-scatter.41
  664.3 30.8 reduce-scatter.43
  698.6 26.8 reduce-scatter.63
  728.4 37.3 reduce-scatter.47
  769.4 40.1 reduce-scatter.55
  812.8 40.1 reduce-scatter.53
  856.5 28.5 reduce-scatter.61
  888.1 42.2 reduce-scatter.51
  933.5 42.2 reduce-scatter.49
  978.0 31.0 reduce-scatter.65
  1012.1 35.5 reduce-scatter.45
  1050.7 52.1 reduce-scatter.59
  1105.8 52.1 reduce-scatter.57
where the time goes:
time: 1170 us
  waiting for transfers between devices  622 us (53%)
  blocking collectives  367 us (31%)
  matrix products  62.6 us (5%)
  local copies, waits for them, and re-layouts  56.6 us (5%)
  other arithmetic  42.3 us (4%)
  between operations  16.4 us (1%)
    reduce_scatter x6, waiting for transfers between devices, weight_grad(): lax.psum_scatter(lax.dot_general(gathered, grad_rows, (((0,), (0,)), ((),...  244 us
    reduce_scatter x8, waiting for transfers between devices, scattered_grad(): return lax.psum_scatter(partials, 'col', scatter_dimension=1, tiled=True)  215 us
    unnamed x32, waiting for transfers between devices  150 us
    all_gather x6, blocking collectives, gather_features(): return lax.all_gather(pieces, 'col', axis=1, tiled=True)  97.1 us
    all_gather x4, blocking collectives, forward_product(): lax.all_gather(weight, 'row', axis=0, tiled=True)  63.8 us
    psum x4, blocking collectives, normalize(): average = lax.psum(jnp.sum(stream, 1, keepdims=True), 'col') / D  61 us
    psum x4, blocking collectives, normalize_back(): lax.psum((jnp.sum(grad_normed, 1, keepdims=True), jnp.sum(grad_normed * n...  56.8 us
    psum x4, blocking collectives, normalize(): spread = lax.psum(jnp.sum(centred * centred, 1, keepdims=True), 'col') / D  55 us
  transfers between devices with their start and end apart: 27, of which 18 were waited for; matrix products, arithmetic and copies ran while one was open for 9% of the time, Pallas kernels for 0%

commit v1 on v0

v1 whole, which is shorter than its diff:
```python
import functools
import math

import jax
import jax.numpy as jnp
from jax import lax
from jax.experimental import pallas as pl
from jax.experimental.pallas import tpu as pltpu
from jax.sharding import PartitionSpec as P

D = 1152
HEAD = 72
LAYERS = 2
EPS = 1e-06
SCALE = HEAD ** (-0.5)
BF16 = jnp.bfloat16
F32 = jnp.float32
MESH = pl.DeviceIdType.MESH
VMEM_BYTES = 52 * 1024 * 1024


def nn(a, b):
    return lax.dot_general(a, b, (((1,), (0,)), ((), ())), preferred_element_type=F32)


def tn(a, b):
    return lax.dot_general(a, b, (((0,), (0,)), ((), ())), preferred_element_type=F32)


def nt(a, b):
    return lax.dot_general(a, b, (((1,), (1,)), ((), ())), preferred_element_type=F32)


def flat(x):
    blocks, rows, columns = x.shape
    if rows % 16 == 0:
        return x.reshape(blocks * rows, columns)
    return x.astype(F32).reshape(blocks * rows, columns).astype(x.dtype)


class Place:
    def __init__(self, count):
        self.row = lax.axis_index("row")
        self.col = lax.axis_index("col")
        self.count = count
        self.zs = count // 2
        self.z = self.col // 2
        self.core = self.col % 2
        self.mate_core = 1 - self.core
        self.mate = (self.row, self.z * 2 + self.mate_core)

    def ahead(self, k):
        return lax.rem(self.z + k, self.zs)

    def behind(self, k):
        return lax.rem(self.z + self.zs - k, self.zs)

    def peer(self, z):
        return (self.row, z * 2 + self.core)


def greet(here):
    barrier = pltpu.get_barrier_semaphore()
    pl.semaphore_signal(barrier, inc=1, device_id=here.mate, device_id_type=MESH)
    for k in range(1, here.zs):
        pl.semaphore_signal(
            barrier, inc=1, device_id=here.peer(here.ahead(k)), device_id_type=MESH
        )
    pl.semaphore_wait(barrier, here.zs)


def send(src, dst, send_sem, recv_sem, device):
    return pltpu.make_async_remote_copy(
        src_ref=src,
        dst_ref=dst,
        send_sem=send_sem,
        recv_sem=recv_sem,
        device_id=device,
        device_id_type=MESH,
    )


def gather(here, buf, out_sem, fwd_sem, in_sem):
    own = here.col
    started = []
    for k in range(1, here.zs):
        copy = send(
            buf.at[own], buf.at[own], out_sem.at[k], in_sem.at[own], here.peer(here.ahead(k))
        )
        copy.start()
        started.append(copy)
    copy = send(buf.at[own], buf.at[own], out_sem.at[0], in_sem.at[own], here.mate)
    copy.start()
    started.append(copy)
    for k in range(1, here.zs):
        src = here.behind(k) * 2 + here.core
        copy = send(buf.at[src], buf.at[src], fwd_sem.at[k], in_sem.at[src], here.mate)
        copy.wait_recv()
        copy.start()
        started.append(copy)
    for k in range(here.zs):
        src = here.behind(k) * 2 + here.mate_core
        send(buf.at[src], buf.at[src], fwd_sem.at[0], in_sem.at[src], here.mate).wait_recv()
    for copy in started:
        copy.wait_send()


def scatter_sum(here, parts, near, far, near_sems, far_sems, stat=None):
    near_out, near_in = near_sems
    far_out, far_in = far_sems
    z, core = here.z, here.core
    order = list(range(1, here.zs)) + [0]
    near_copies = []
    if stat is not None:
        own, got, sums, others, stat_sems = stat
        stat_out, stat_in = stat_sems
        first = send(own, got, stat_out.at[0], stat_in.at[z], here.mate)
        first.start()
    for k in order:
        to = here.ahead(k)
        copy = send(
            parts.at[here.mate_core, to], near.at[to], near_out.at[k], near_in.at[to], here.mate
        )
        copy.start()
        near_copies.append(copy)
    far_copies = []
    if stat is not None:
        first.wait()
        sums[...] = own[...] + got[...]
        for k in range(1, here.zs):
            copy = send(
                sums, others.at[z], stat_out.at[k], stat_in.at[z], here.peer(here.ahead(k))
            )
            copy.start()
            far_copies.append(copy)
    total = None
    for i, k in enumerate(order):
        to = here.ahead(k)
        near_copies[i].wait_recv()
        both = parts[core, to].astype(F32) + near[to].astype(F32)
        if k == 0:
            total = both
        else:
            parts[core, to] = both.astype(BF16)
            copy = send(
                parts.at[core, to], far.at[z], far_out.at[k], far_in.at[z], here.peer(to)
            )
            copy.start()
            far_copies.append(copy)
    stat_total = None
    if stat is not None:
        stat_total = sums[...]
        for k in range(1, here.zs):
            src = here.behind(k)
            send(
                sums, others.at[src], stat_out.at[k], stat_in.at[src], here.peer(src)
            ).wait_recv()
            stat_total = stat_total + others[src]
    for k in range(1, here.zs):
        src = here.behind(k)
        send(
            parts.at[core, src], far.at[src], far_out.at[k], far_in.at[src], here.peer(src)
        ).wait_recv()
        total = total + far[src].astype(F32)
    for copy in near_copies:
        copy.wait_send()
    for copy in far_copies:
        copy.wait_send()
    return total, stat_total


def normalize(stream):
    average = jnp.sum(stream, 0, keepdims=True) / D
    centred = stream - average
    spread = jnp.sum(centred * centred, 0, keepdims=True) / D
    inverse = lax.rsqrt(spread + EPS)
    return centred * inverse, inverse


def gelu(u):
    inner = math.sqrt(2 / math.pi) * (u + 0.044715 * (u * u * u))
    return 0.5 * u * (1.0 + jnp.tanh(inner))


def gelu_slope(u):
    root = math.sqrt(2 / math.pi)
    t = jnp.tanh(root * (u + 0.044715 * (u * u * u)))
    return 0.5 * (1.0 + t) + 0.5 * u * (1.0 - t * t) * (root * (1.0 + 3 * 0.044715 * (u * u)))


def attention_forward(
    count, stream, mod, mod_own, w_qkv, b_qkv, w_out, b_out,
    normed, inverse, hidden, qkv, log_total, attended, branch, stream_out,
    x_buf, a_buf, x_out, x_fwd, x_in, a_out, a_fwd, a_in,
):
    here = Place(count)
    greet(here)
    x_buf[here.col] = stream[...].astype(BF16)
    gather(here, x_buf, x_out, x_fwd, x_in)
    values, inv = normalize(flat(x_buf[...]).astype(F32))
    normed[...] = values
    inverse[...] = inv
    hidden_now = (values * (1.0 + mod[:, 1:2]) + mod[:, 0:1]).astype(BF16)
    hidden[...] = hidden_now
    projected = tn(flat(w_qkv[...]), hidden_now) + b_qkv[...]
    heads = qkv.shape[0] // 3
    for i in range(3 * heads):
        qkv[i] = projected[i * HEAD : (i + 1) * HEAD].astype(BF16)
    pieces = []
    for h in range(heads):
        scores = tn(qkv[heads + h], qkv[h]) * SCALE
        highest = jnp.max(scores, axis=0, keepdims=True)
        expd = jnp.exp(scores - highest)
        summed = jnp.sum(expd, axis=0, keepdims=True)
        log_total[h] = highest + jnp.log(summed)
        probs = (expd / summed).astype(BF16)
        pieces.append(nn(qkv[2 * heads + h], probs))
    a_buf[here.col] = jnp.concatenate(pieces, axis=0).astype(BF16)
    gather(here, a_buf, a_out, a_fwd, a_in)
    attended_now = flat(a_buf[...])
    attended[...] = attended_now
    branch_now = tn(flat(w_out[...]), attended_now) + b_out[...]
    branch[...] = branch_now
    stream_out[...] = stream[...] + mod_own[:, 2:3] * branch_now


def mlp_forward(
    count, stream, mod, mod_own, w_one, b_one, w_two, b_two,
    normed, inverse, hidden, pre, activated, branch, stream_out,
    x_buf, a_buf, x_out, x_fwd, x_in, a_out, a_fwd, a_in,
):
    here = Place(count)
    greet(here)
    x_buf[here.col] = stream[...].astype(BF16)
    gather(here, x_buf, x_out, x_fwd, x_in)
    values, inv = normalize(flat(x_buf[...]).astype(F32))
    normed[...] = values
    inverse[...] = inv
    hidden_now = (values * (1.0 + mod[:, 4:5]) + mod[:, 3:4]).astype(BF16)
    hidden[...] = hidden_now
    pre_now = tn(flat(w_one[...]), hidden_now) + b_one[...]
    pre[...] = pre_now
    a_buf[here.col] = gelu(pre_now).astype(BF16)
    gather(here, a_buf, a_out, a_fwd, a_in)
    activated_now = flat(a_buf[...])
    activated[...] = activated_now
    branch_now = tn(flat(w_two[...]), activated_now) + b_two[...]
    branch[...] = branch_now
    stream_out[...] = stream[...] + mod_own[:, 5:6] * branch_now


def split_parts(here, parts, weight, rows):
    for c in range(here.count):
        parts[c % 2, c // 2] = nn(weight[c], rows).astype(BF16)


def split_norm_parts(here, parts, stat, weight, rows, normed, gain):
    width = weight.shape[1]
    plain = crossed = 0.0
    for c in range(here.count):
        block = nn(weight[c], rows)
        parts[c % 2, c // 2] = block.astype(BF16)
        span = slice(c * width, (c + 1) * width)
        scaled = block * (1.0 + gain[span])
        plain = plain + jnp.sum(scaled, 0, keepdims=True)
        crossed = crossed + jnp.sum(scaled * normed[span], 0, keepdims=True)
    stat[0:1] = plain
    stat[1:2] = crossed


def norm_back(here, grad_hidden, totals, normed, inverse, gain):
    width = grad_hidden.shape[0]
    own = normed[pl.ds(pl.multiple_of(here.col * width, 8), width)]
    scaled = grad_hidden * (1.0 + gain)
    change = inverse[...] * (scaled - totals[0:1] / D - own * (totals[1:2] / D))
    shift = jnp.sum(grad_hidden, 1, keepdims=True)
    stretch = jnp.sum(grad_hidden * own, 1, keepdims=True)
    return change, shift, stretch


def mlp_backward(
    count, grad, mod, mod_own, branch, pre, normed, inverse, w_one, w_two,
    grad_branch, grad_pre, grad_out, sums, sums_pre,
    a_parts, a_near, a_far, h_parts, h_near, h_far, stat_own, stat_got, stat_sum, stat_far,
    an_out, an_in, af_out, af_in, hn_out, hn_in, hf_out, hf_in, st_out, st_in,
):
    here = Place(count)
    greet(here)
    grad_now = grad[...]
    grad_branch_now = (mod_own[:, 5:6] * grad_now).astype(BF16)
    grad_branch[...] = grad_branch_now
    split_parts(here, a_parts, w_two, grad_branch_now)
    grad_act, _ = scatter_sum(
        here, a_parts, a_near, a_far, (an_out, an_in), (af_out, af_in)
    )
    grad_pre_now = (grad_act * gelu_slope(pre[...])).astype(BF16)
    grad_pre[...] = grad_pre_now
    stat_own[...] = jnp.zeros_like(stat_own)
    split_norm_parts(here, h_parts, stat_own, w_one, grad_pre_now, normed, mod[:, 4:5])
    grad_hidden, totals = scatter_sum(
        here, h_parts, h_near, h_far, (hn_out, hn_in), (hf_out, hf_in),
        (stat_own, stat_got, stat_sum, stat_far, (st_out, st_in)),
    )
    change, shift, stretch = norm_back(
        here, grad_hidden, totals, normed, inverse, mod_own[:, 4:5]
    )
    grad_out[...] = grad_now + change
    sums[:, 0:1] = shift
    sums[:, 1:2] = stretch
    sums[:, 2:3] = jnp.sum(grad_now * branch[...], 1, keepdims=True)
    sums[:, 3:4] = jnp.sum(grad_branch_now.astype(F32), 1, keepdims=True)
    sums_pre[...] = jnp.sum(grad_pre_now.astype(F32), 1, keepdims=True)


def attention_backward(
    count, grad, mod, mod_own, branch, qkv, log_total, normed, inverse, w_qkv, w_out,
    grad_branch, grad_qkv, grad_out, sums, sums_qkv,
    a_parts, a_near, a_far, h_parts, h_near, h_far, stat_own, stat_got, stat_sum, stat_far,
    an_out, an_in, af_out, af_in, hn_out, hn_in, hf_out, hf_in, st_out, st_in,
):
    here = Place(count)
    greet(here)
    grad_now = grad[...]
    grad_branch_now = (mod_own[:, 2:3] * grad_now).astype(BF16)
    grad_branch[...] = grad_branch_now
    split_parts(here, a_parts, w_out, grad_branch_now)
    grad_att, _ = scatter_sum(
        here, a_parts, a_near, a_far, (an_out, an_in), (af_out, af_in)
    )
    heads = qkv.shape[0] // 3
    queries, keys, values = [], [], []
    for h in range(heads):
        query, key, value = qkv[h], qkv[heads + h], qkv[2 * heads + h]
        grad_one = grad_att[h * HEAD : (h + 1) * HEAD].astype(BF16)
        weights = jnp.exp(tn(key, query) * SCALE - log_total[h])
        grad_weights = tn(value, grad_one)
        values.append(nt(grad_one, weights.astype(BF16)))
        inner = jnp.sum(weights * grad_weights, axis=0, keepdims=True)
        grad_scores = (weights * (grad_weights - inner)).astype(BF16)
        queries.append(nn(key, grad_scores) * SCALE)
        keys.append(nt(query, grad_scores) * SCALE)
    grad_qkv_now = jnp.concatenate(queries + keys + values, axis=0).astype(BF16)
    grad_qkv[...] = grad_qkv_now
    stat_own[...] = jnp.zeros_like(stat_own)
    split_norm_parts(here, h_parts, stat_own, w_qkv, grad_qkv_now, normed, mod[:, 1:2])
    grad_hidden, totals = scatter_sum(
        here, h_parts, h_near, h_far, (hn_out, hn_in), (hf_out, hf_in),
        (stat_own, stat_got, stat_sum, stat_far, (st_out, st_in)),
    )
    change, shift, stretch = norm_back(
        here, grad_hidden, totals, normed, inverse, mod_own[:, 1:2]
    )
    grad_out[...] = grad_now + change
    sums[:, 0:1] = shift
    sums[:, 1:2] = stretch
    sums[:, 2:3] = jnp.sum(grad_now * branch[...], 1, keepdims=True)
    sums[:, 3:4] = jnp.sum(grad_branch_now.astype(F32), 1, keepdims=True)
    sums_qkv[...] = jnp.sum(grad_qkv_now.astype(F32), 1, keepdims=True)


def run(body, ident, count, args, outs, scratch):
    vmem = pl.BlockSpec(memory_space=pltpu.VMEM)
    return pl.pallas_call(
        functools.partial(body, count),
        out_shape=[jax.ShapeDtypeStruct(shape, dtype) for shape, dtype in outs],
        in_specs=[vmem] * len(args),
        out_specs=[vmem] * len(outs),
        scratch_shapes=scratch,
        compiler_params=pltpu.CompilerParams(
            collective_id=ident, has_side_effects=True, vmem_limit_bytes=VMEM_BYTES
        ),
        cost_estimate=pl.CostEstimate(
            flops=2_000_000_000, bytes_accessed=60_000_000, transcendentals=0
        ),
    )(*args)


def gather_scratch(count, sizes, width):
    bufs = [pltpu.VMEM((count, size, width), BF16) for size in sizes]
    sems = [pltpu.SemaphoreType.DMA((count,)) for _ in range(3 * len(sizes))]
    return bufs + sems


def scatter_scratch(count, sizes, width):
    zs = count // 2
    bufs = []
    for size in sizes:
        bufs.append(pltpu.VMEM((2, zs, size, width), BF16))
        bufs.append(pltpu.VMEM((zs, size, width), BF16))
        bufs.append(pltpu.VMEM((zs, size, width), BF16))
    bufs += [pltpu.VMEM((8, width), F32) for _ in range(3)]
    bufs.append(pltpu.VMEM((zs, 8, width), F32))
    sems = [pltpu.SemaphoreType.DMA((zs,)) for _ in range(4 * len(sizes) + 2)]
    return bufs + sems


def weight_grad(gathered, grad_rows):
    product = lax.dot_general(
        gathered, grad_rows, (((1,), (1,)), ((), ())), preferred_element_type=F32
    )
    return lax.psum_scatter(
        product.astype(BF16), "row", scatter_dimension=0, tiled=True
    ).astype(F32)


def whole_rows(weight, count):
    full = lax.all_gather(weight, "row", axis=0, tiled=True)
    return full.reshape(count, full.shape[0] // count, full.shape[1])


def per_device(
    count,
    tokens, cond, w_mod, b_mod, query_key_value_weight, b_qv,
    attention_output_weight, attention_output_bias, first_linear_weight, first_linear_bias,
    second_linear_weight, second_linear_bias, cotangent,
):
    seq_count = cond.shape[0]
    assert seq_count == 1
    length, width = tokens.shape
    heads = width // HEAD
    hidden_width = first_linear_weight.shape[2]
    rows_in = w_mod.shape[1]
    row_index = lax.axis_index("row")
    cond_float = cond.astype(F32)
    signal = jax.nn.silu(cond_float).astype(BF16)
    signal_all = lax.all_gather(
        lax.all_gather(signal, "col", axis=1, tiled=True), "row", axis=0, tiled=True
    )
    signal_part = lax.dynamic_slice_in_dim(signal_all, row_index * rows_in, rows_in, 1)
    mod_parts = jnp.stack(
        [
            jnp.dot(signal_part, w_mod[i].reshape(rows_in, -1), preferred_element_type=F32)
            for i in range(LAYERS)
        ],
        axis=1,
    )
    mod_own = lax.psum_scatter(mod_parts, "row", scatter_dimension=0, tiled=True)
    mod_own = mod_own.reshape(LAYERS, 6, width) + b_mod
    mod_own = jnp.swapaxes(mod_own, 1, 2)
    mod_full = lax.all_gather(mod_own, "col", axis=1, tiled=True)

    weights = []
    for i in range(LAYERS):
        weights.append(
            (
                whole_rows(query_key_value_weight[i].reshape(rows_in, -1), count),
                whole_rows(attention_output_weight[i], count),
                whole_rows(first_linear_weight[i], count),
                whole_rows(second_linear_weight[i], count),
            )
        )

    stream = tokens.astype(F32).T
    saved = []
    for i in range(LAYERS):
        w_qkv, w_out, w_one, w_two = weights[i]
        bias = jnp.concatenate([b_qv[i, 0], jnp.zeros_like(b_qv[i, 0]), b_qv[i, 1]])[:, None]
        normed1, inverse1, hidden1, qkv, log_total, attended, branch1, stream = run(
            attention_forward, 0, count,
            (
                stream, mod_full[i], mod_own[i], w_qkv, bias, w_out,
                attention_output_bias[i][:, None],
            ),
            [
                ((D, length), F32),
                ((1, length), F32),
                ((D, length), BF16),
                ((3 * heads, HEAD, length), BF16),
                ((heads, 1, length), F32),
                ((D, length), BF16),
                ((width, length), F32),
                ((width, length), F32),
            ],
            gather_scratch(count, (width, width), length),
        )
        normed2, inverse2, hidden2, pre, activated, branch2, stream = run(
            mlp_forward, 1, count,
            (
                stream, mod_full[i], mod_own[i], w_one, first_linear_bias[i][:, None], w_two,
                second_linear_bias[i][:, None],
            ),
            [
                ((D, length), F32),
                ((1, length), F32),
                ((D, length), BF16),
                ((hidden_width, length), F32),
                ((count * hidden_width, length), BF16),
                ((width, length), F32),
                ((width, length), F32),
            ],
            gather_scratch(count, (width, hidden_width), length),
        )
        saved.append(
            (
                normed1, inverse1, hidden1, qkv, log_total, attended, branch1,
                normed2, inverse2, hidden2, pre, activated, branch2,
            )
        )
    output = stream.T.astype(BF16)

    grad = cotangent.astype(F32).T
    signal_back = jnp.zeros((signal_all.shape[0], rows_in), F32)
    results = {}
    for i in reversed(range(LAYERS)):
        w_qkv, w_out, w_one, w_two = weights[i]
        (
            normed1, inverse1, hidden1, qkv, log_total, attended, branch1,
            normed2, inverse2, hidden2, pre, activated, branch2,
        ) = saved[i]
        grad_branch2, grad_pre, grad, sums2, sums_pre = run(
            mlp_backward, 2, count,
            (grad, mod_full[i], mod_own[i], branch2, pre, normed2, inverse2, w_one, w_two),
            [
                ((width, length), BF16),
                ((hidden_width, length), BF16),
                ((width, length), F32),
                ((width, 4), F32),
                ((hidden_width, 1), F32),
            ],
            scatter_scratch(count, (hidden_width, width), length),
        )
        grad_fc2 = weight_grad(activated, grad_branch2)
        grad_fc1 = weight_grad(hidden2, grad_pre)
        grad_branch1, grad_qkv, grad, sums1, sums_qkv = run(
            attention_backward, 3, count,
            (
                grad, mod_full[i], mod_own[i], branch1, qkv, log_total, normed1, inverse1,
                w_qkv, w_out,
            ),
            [
                ((width, length), BF16),
                ((3 * width, length), BF16),
                ((width, length), F32),
                ((width, 4), F32),
                ((3 * width, 1), F32),
            ],
            scatter_scratch(count, (width, width), length),
        )
        grad_out_w = weight_grad(attended, grad_branch1)
        grad_qkv_w = weight_grad(hidden1, grad_qkv).reshape(-1, 3, width)
        grad_mod = jnp.concatenate([sums1[:, 0:3], sums2[:, 0:3]], axis=1).T.astype(BF16)
        grad_mod_all = lax.all_gather(
            grad_mod.reshape(1, 6 * width), "row", axis=0, tiled=True
        )
        grad_mod_w = lax.dot_general(
            signal_part, grad_mod_all, (((0,), (0,)), ((), ())), preferred_element_type=F32
        ).reshape(-1, 6, width)
        signal_back = signal_back + lax.dot_general(
            grad_mod_all,
            w_mod[i].reshape(rows_in, -1),
            (((1,), (1,)), ((), ())),
            preferred_element_type=F32,
        )
        bias_mod = jnp.sum(grad_mod_all.astype(F32), 0).reshape(6, width)
        biases = (
            jnp.stack([sums_qkv[:width, 0], sums_qkv[2 * width :, 0]]),
            sums1[:, 3],
            sums_pre[:, 0],
            sums2[:, 3],
        )
        results[i] = (grad_mod_w, bias_mod, grad_qkv_w, grad_out_w, grad_fc1, grad_fc2, biases)
    bias_sums = lax.psum([results[i][6] for i in range(LAYERS)], "row")
    signal_back = lax.psum(signal_back, "col")
    signal_back = lax.all_gather(signal_back, "row", axis=1, tiled=True)
    grad_signal = lax.dynamic_slice(
        signal_back,
        (row_index * seq_count, lax.axis_index("col") * width),
        (seq_count, width),
    )
    grad_cond = jax.vjp(jax.nn.silu, cond_float)[1](grad_signal)[0]

    def stacked(member):
        return jnp.stack([results[i][member] for i in range(LAYERS)])

    def stacked_bias(member):
        return jnp.stack([bias_sums[i][member] for i in range(LAYERS)])

    return (
        output,
        grad.T,
        grad_cond,
        stacked(0),
        stacked(1),
        stacked(2),
        stacked_bias(0),
        stacked(3),
        stacked_bias(1),
        stacked(4),
        stacked_bias(2),
        stacked(5),
        stacked_bias(3),
    )


def solution(mesh):
    in_specs = (
        P("row", "col"),
        P("row", "col"),
        P(None, "row", None, "col"),
        P(None, None, "col"),
        P(None, "row", None, "col"),
        P(None, None, "col"),
        P(None, "row", "col"),
        P(None, "col"),
        P(None, "row", "col"),
        P(None, "col"),
        P(None, "row", "col"),
        P(None, "col"),
        P("row", "col"),
    )
    out_specs = (
        P("row", "col"),
        P("row", "col"),
        P("row", "col"),
        P(None, "row", None, "col"),
        P(None, None, "col"),
        P(None, "row", None, "col"),
        P(None, None, "col"),
        P(None, "row", "col"),
        P(None, "col"),
        P(None, "row", "col"),
        P(None, "col"),
        P(None, "row", "col"),
        P(None, "col"),
    )
    return jax.shard_map(
        functools.partial(per_device, mesh.shape["col"]),
        mesh=mesh,
        in_specs=in_specs,
        out_specs=out_specs,
        check_vma=False,
    )
```

time: 1170 us -> 717 us (0.61)
  waiting for transfers between devices: 622 us -> 146 us
  Pallas kernels: 0 us -> 282 us
  blocking collectives: 367 us -> 189 us
  matrix products: 62.6 us -> 16 us
  other arithmetic: 42.3 us -> 12 us
    reduce_scatter x14 -> x4, waiting for transfers between devices: 459 us -> 68.1 us  [weight_grad(): lax.psum_scatter(product.astype(BF16), 'row', scatter_dimension=0, tiled=...]
    pallas_call x0 -> x8, Pallas kernels: none -> 282 us  [run(): pl.pallas_call(functools.partial(body, count), out_shape=[jax.ShapeDtypeS...]
    psum x13 -> x2, blocking collectives: 188 us -> 29.9 us  [the longest x1 15.3 us: per_device(): bias_sums = lax.psum([results[i][6] for i in range(LAYERS)], 'row')]
    unnamed x32 -> x16, waiting for transfers between devices: 150 us -> 77.5 us
    dot_general x38 -> x14, matrix products: 59.9 us -> 16 us  [the longest x8 14.3 us: weight_grad(): lax.dot_general(gathered, grad_rows, (((1,), (1,)), ((), ())), preferred_...]
    all_gather x10 -> x9, blocking collectives: 161 us -> 126 us  [the longest x4 76.8 us: whole_rows(): full = lax.all_gather(weight, 'row', axis=0, tiled=True)]
    unnamed x0 -> x2, blocking collectives: none -> 33.6 us
    reshape x1 -> x0, blocking collectives: 18.1 us -> none
  transfers between devices with their start and end apart: 27 -> 12, of which waited for: 18 -> 5; matrix products, arithmetic and copies ran while one was open for 9% -> 8% of each run, Pallas kernels for 0% -> 23%
where the time goes in v1:
time: 717 us; the launch traced here: 716 us
  Pallas kernels  282 us (39%)
  blocking collectives  189 us (26%)
  waiting for transfers between devices  146 us (20%)
  local copies, waits for them, and re-layouts  55.2 us (8%)
  matrix products  16 us (2%)
  between operations  15.9 us (2%)
  other arithmetic  12 us (2%)
    pallas_call x8, Pallas kernels, run(): pl.pallas_call(functools.partial(body, count), out_shape=[jax.ShapeDtypeS...  282 us
    unnamed x16, waiting for transfers between devices  77.5 us
    all_gather x4, blocking collectives, whole_rows(): full = lax.all_gather(weight, 'row', axis=0, tiled=True)  76.8 us
    reduce_scatter x4, waiting for transfers between devices, weight_grad(): lax.psum_scatter(product.astype(BF16), 'row', scatter_dimension=0, tiled=...  68.1 us
    unnamed x170, local copies, waits for them, and re-layouts  38.2 us
    unnamed x2, blocking collectives  33.6 us
    all_gather x1, blocking collectives, per_device(): mod_full = lax.all_gather(mod_own, 'col', axis=1, tiled=True)  16.8 us
    all_gather x2, blocking collectives, per_device(): lax.all_gather(grad_mod.reshape(1, 6 * width), 'row', axis=0, tiled=True)  15.4 us
  transfers between devices with their start and end apart: 12, of which 5 were waited for; matrix products, arithmetic and copies ran while one was open for 8% of the time, Pallas kernels for 23%

profile of v1, /device:TPU:0, one launch (start us, length us, event | category | flops | bytes accessed | tf_op | source)
XLA Modules:
  0.0 716.3 jit_solution(15576220175278988356)
XLA Ops:
  14.5 18.1 %all-reduce = bf16[1152]{0:T(1024)(128)(2,1)S(1)} all-reduce(bf16[1152]{0:T(1024)(128)(2,1)S(1)} %dynamic-update-slice), channel_id=1, replica_groups=mesh['row'=4,'col'=8] {'col'}, use_global_device_ids=true, to_apply=%add | all-reduce | flops 1152 | bytes 4608
  32.6 8.4 %all-gather.6 = bf16[4,1,1152]{2,1,0:T(2,128)(2,1)S(1)} all-gather(bf16[1,1,1152]{2,1,0:T(2,128)(2,1)S(1)} %reshape.91), channel_id=1, replica_groups=mesh['row'=4,'col'=8] {'row'}, dimensions={0}, use_global_device_ids=true | all-gather | bytes 11520 | tf_op jit(solution)/shard_map/all_gather | solution.py:426
  41.7 15.5 %all-reduce.1 = f32[4,2,864]{2,1,0:T(2,128)S(1)} all-reduce(f32[4,2,864]{2,1,0:T(2,128)S(1)} %copy.121), channel_id=8, replica_groups=mesh['row'=4,'col'=8] {'row'}, use_global_device_ids=true, to_apply=%region_0.1.clone | all-reduce | flops 6912 | bytes 55296
  59.0 21.4 %all_gather.45 = bf16[1152,432]{1,0:T(8,128)(2,1)} all-gather(bf16[288,432]{1,0:T(8,128)(2,1)S(1)} %copy.124), channel_id=1, replica_groups=mesh['row'=4,'col'=8] {'row'}, dimensions={0}, use_global_device_ids=true | all-gather | bytes 1244160 | tf_op jit(solution)/shard_map/all_gather | solution.py:407
  80.9 17.8 %all-gather = bf16[1,1152,144]{2,0,1:T(2,128)(2,1)S(1)} all-gather(bf16[1,288,144]{2,0,1:T(2,128)(2,1)S(1)} %copy.171), channel_id=2, replica_groups=mesh['row'=4,'col'=8] {'row'}, dimensions={1}, use_global_device_ids=true | all-gather | bytes 414720 | tf_op jit(solution)/shard_map/all_gather | solution.py:407
  100.6 17.9 %all-gather.3 = bf16[1,1152,144]{2,0,1:T(2,128)(2,1)S(1)} all-gather(bf16[1,288,144]{2,0,1:T(2,128)(2,1)S(1)} %copy.172), channel_id=5, replica_groups=mesh['row'=4,'col'=8] {'row'}, dimensions={1}, use_global_device_ids=true | all-gather | bytes 414720 | tf_op jit(solution)/shard_map/all_gather | solution.py:407
  119.8 16.8 %all_gather.44 = f32[2,1152,6]{2,1,0:T(8,128)S(1)} all-gather(f32[2,144,6]{2,1,0:T(8,128)S(1)} %bitcast.148), channel_id=1, replica_groups=mesh['row'=4,'col'=8] {'col'}, dimensions={1}, use_global_device_ids=true | all-gather | bytes 62208 | tf_op jit(solution)/shard_map/all_gather | solution.py:440
  136.6 19.7 %all_gather.49 = bf16[1152,432]{1,0:T(8,128)(2,1)} all-gather(bf16[288,432]{1,0:T(8,128)(2,1)S(1)} %copy.133), channel_id=1, replica_groups=mesh['row'=4,'col'=8] {'row'}, dimensions={0}, use_global_device_ids=true | all-gather | bytes 1244160 | tf_op jit(solution)/shard_map/all_gather | solution.py:407
  157.5 23.4 %shard_map.228 = (f32[1152,256]{1,0:T(8,128)}, f32[1,256]{1,0:T(1,128)S(1)}, bf16[1152,256]{1,0:T(8,128)(2,1)S(1)}, bf16[6,72,256]{2,1,0:T(8,128)(2,1)S(1)}, f32...) custom-call(f32[144,256]{1,0:T(8,128)S(1)} %convert_bitcast_fusion.1.stream,, ...), custom_call_target="tpu_custom_call" | custom-call | flops 2000000000 | bytes 60000000 | tf_op jit(solution)/shard_map/pallas_call | solution.py:363
  182.3 3.8 copy.130
  186.1 3.8 copy.139
  189.9 41.8 %shard_map.229 = (f32[1152,256]{1,0:T(8,128)}, f32[1,256]{1,0:T(1,128)S(1)}, bf16[1152,256]{1,0:T(8,128)(2,1)S(1)}, f32[576,256]{1,0:T(8,128)}, bf16[4608,256]{1...) custom-call(f32[144,256]{1,0:T(8,128)S(1)} %get-tuple-element.63.stream, ...), custom_call_target="tpu_custom_call" | custom-call | flops 2000000000 | bytes 60000000 | tf_op jit(solution)/shard_map/pallas_call | solution.py:363
  232.3 29.6 %shard_map.230 = (f32[1152,256]{1,0:T(8,128)}, f32[1,256]{1,0:T(1,128)S(1)}, bf16[1152,256]{1,0:T(8,128)(2,1)S(1)}, bf16[6,72,256]{2,1,0:T(8,128)(2,1)S(1)}, f32...) custom-call(f32[144,256]{1,0:T(8,128)S(1)} %get-tuple-element.64.stream, ...), custom_call_target="tpu_custom_call" | custom-call | flops 2000000000 | bytes 60000000 | tf_op jit(solution)/shard_map/pallas_call | solution.py:363
  265.4 42.0 %shard_map.231 = (f32[1152,256]{1,0:T(8,128)}, f32[1,256]{1,0:T(1,128)S(1)}, bf16[1152,256]{1,0:T(8,128)(2,1)S(1)}, f32[576,256]{1,0:T(8,128)}, bf16[4608,256]{1...) custom-call(f32[144,256]{1,0:T(8,128)S(1)} %copy-done.38, f32[1152,6]{1,0:T(8,128)} %get-tuple-element.181.mod, ...), custom_call_target="tpu_custom_call" | custom-call | flops 2000000000 | bytes 60000000 | tf_op jit(solution)/shard_map/pallas_call | solution.py:363
  307.4 49.9 %shard_map.232 = (bf16[144,256]{1,0:T(8,128)(2,1)S(1)}, bf16[576,256]{1,0:T(8,128)(2,1)S(1)}, f32[144,256]{1,0:T(8,128)S(1)}, f32[144,4]{1,0:T(8,128)S(1)}, f32[576,1]{1,0:T(8,128)S(1)}) custom-call(f32[144,256]{1,0:T(8,128)S(1)} %convert_bitcast_fusion.grad, f32[1152,6]{1,0:T(8,128)S(1)} %copy-done.1, f32[144,6]{1,0:T(8,128)S(1)} %get-tuple-element.191.mod_own, ...), custom_call_target="tpu_custom_call" | custom-call | flops 2000000000 | bytes 60000000 | tf_op jit(solution)/shard_map/pallas_call | solution.py:363
  358.2 23.7 %shard_map.233 = (bf16[144,256]{1,0:T(8,128)(2,1)S(1)}, bf16[432,256]{1,0:T(8,128)(2,1)S(1)}, f32[144,256]{1,0:T(8,128)S(1)}, f32[144,4]{1,0:T(8,128)S(1)}, f32[432,1]{1,0:T(8,128)S(1)}) custom-call(f32[144,256]{1,0:T(8,128)S(1)} %get-tuple-element.71.grad, f32[1152,6]{1,0:T(8,128)S(1)} %copy-done.1, f32[144,6]{1,0:T(8,128)S(1)} %get-tuple-element.191.mod_own, ...), custom_call_target="tpu_custom_call" | custom-call | flops 2000000000 | bytes 60000000 | tf_op jit(solution)/shard_map/pallas_call | solution.py:363
  390.6 48.1 %shard_map.234 = (bf16[144,256]{1,0:T(8,128)(2,1)S(1)}, bf16[576,256]{1,0:T(8,128)(2,1)S(1)}, f32[144,256]{1,0:T(8,128)S(1)}, f32[144,4]{1,0:T(8,128)S(1)}, f32[576,1]{1,0:T(8,128)S(1)}) custom-call(f32[144,256]{1,0:T(8,128)S(1)} %copy-done.36, f32[1152,6]{1,0:T(8,128)S(1)} %copy-done, f32[144,6]{1,0:T(8,128)S(1)} %copy-done.27, f32[144,256]{1,0:T(8,128)S(1)} %copy-done.34, ...), custom_call_target="tpu_custom_call" | custom-call | flops 2000000000 | bytes 60000000 | tf_op jit(solution)/shard_map/pallas_call | solution.py:363
  440.1 23.4 %shard_map.235 = (bf16[144,256]{1,0:T(8,128)(2,1)S(1)}, bf16[432,256]{1,0:T(8,128)(2,1)S(1)}, f32[144,256]{1,0:T(8,128)S(1)}, f32[144,4]{1,0:T(8,128)S(1)}, f32[432,1]{1,0:T(8,128)S(1)}) custom-call(f32[144,256]{1,0:T(8,128)S(1)} %get-tuple-element.82.grad, f32[1152,6]{1,0:T(8,128)S(1)} %copy-done, f32[144,6]{1,0:T(8,128)S(1)} %copy-done.28, ...), custom_call_target="tpu_custom_call" | custom-call | flops 2000000000 | bytes 60000000 | tf_op jit(solution)/shard_map/pallas_call | solution.py:363
  471.1 3.6 convolution_convert_fusion
  474.7 3.8 copy.162
  483.8 8.2 %all-gather.7 = bf16[4,1,864]{2,1,0:T(2,128)(2,1)S(1)} all-gather(bf16[1,1,864]{2,1,0:T(2,128)(2,1)S(1)} %reshape.93), channel_id=1, replica_groups=mesh['row'=4,'col'=8] {'row'}, dimensions={0}, use_global_device_ids=true | all-gather | bytes 8640 | tf_op jit(solution)/shard_map/all_gather | solution.py:542
  492.0 7.2 all-gather.8
  499.6 14.6 %psum.63 = f32[4,288]{1,0:T(4,128)S(1)} all-reduce(f32[4,288]{1,0:T(4,128)S(1)} %convolution_add_fusion), channel_id=1, replica_groups=mesh['row'=4,'col'=8] {'col'}, use_global_device_ids=true, to_apply=%region_1.2 | all-reduce | flops 1152 | bytes 9216 | tf_op jit(solution)/shard_map/psum | solution.py:563
  514.2 8.2 %all-gather.9 = f32[4,288,4]{1,2,0:T(4,128)S(1)} all-gather(f32[1,288,4]{1,2,0:T(4,128)S(1)} %bitcast.166), channel_id=1, replica_groups=mesh['row'=4,'col'=8] {'row'}, dimensions={0}, use_global_device_ids=true | all-gather | bytes 23040 | tf_op jit(solution)/shard_map/all_gather | solution.py:564
  523.7 2.6 convolution_convert_fusion.1
  526.3 2.4 copy.160
  530.5 15.3 %all-reduce.2 = (f32[1,2,144]{2,1,0:T(2,128)S(1)}, f32[1,2,144]{2,1,0:T(2,128)S(1)}, f32[1,144]{1,0:T(1,128)S(1)}, f32[1,144]{1,0:T(1,128)S(1)}, f32[1,576]{1,0:...) all-reduce(f32[1,2,144]{2,1,0:T(2,128)S(1)} %maximum_bitcast_fusion, ...), channel_id=1, replica_groups=mesh['row'=4,'col'=8] {'row'}, use_global_device_ids=true, to_apply=%region_7.8 | all-reduce | flops 2304 | bytes 18432 | tf_op jit(solution)/shard_map/psum | solution.py:562
  560.6 38.1 %reduce-scatter.31.cloned.1.call-done = bf16[1152,144]{1,0:T(8,128)(2,1)} async-done(((bf16[4608,144]{1,0:T(8,128)(2,1)}), bf16[1152,144]{1,0:T(8,128)(2,1)}) %reduce-scatter.31.cloned.1.call-update) | async-done | bytes 331792
  599.9 32.5 %reduce-scatter.23.cloned.1.call-done = bf16[288,576]{1,0:T(8,128)(2,1)} async-done(((bf16[1152,576]{1,0:T(8,128)(2,1)}), bf16[288,576]{1,0:T(8,128)(2,1)}) %reduce-scatter.23.cloned.1.call-update) | async-done | bytes 331792 | tf_op jit(solution)/shard_map/reduce_scatter | solution.py:401
  632.4 33.6 %reduce-scatter.21.cloned.1.call-done = bf16[288,576]{1,0:T(8,128)(2,1)} async-done(((bf16[1152,576]{1,0:T(8,128)(2,1)}), bf16[288,576]{1,0:T(8,128)(2,1)}) %reduce-scatter.21.cloned.1.call-update) | async-done | bytes 331792 | tf_op jit(solution)/shard_map/reduce_scatter | solution.py:401
  666.0 2.3 maximum_convert_fusion
  668.3 38.0 %reduce-scatter.29.cloned.1.call-done = bf16[1152,144]{1,0:T(8,128)(2,1)} async-done(((bf16[4608,144]{1,0:T(8,128)(2,1)}), bf16[1152,144]{1,0:T(8,128)(2,1)}) %reduce-scatter.29.cloned.1.call-update) | async-done | bytes 331792
  (278 shorter events, 65.0 us)
Async XLA Ops:
  7.2 175.1 %all-gather.17.cloned.1.call-start = ((), (), s32[]{:S(2)}) async-start(), calls=%async_computation.13 | async-start | bytes 1658880 | tf_op jit(solution)/shard_map/all_gather | solution.py:407
  9.3 176.8 %all-gather.21.cloned.1.call-start = ((), (), s32[]{:S(2)}) async-start(), calls=%async_computation.15 | async-start | bytes 1658880 | tf_op jit(solution)/shard_map/all_gather | solution.py:407
  10.0 179.8 %all-gather.15.cloned.1.call-start = ((), (), s32[]{:S(2)}) async-start(), calls=%async_computation.12 | async-start | bytes 1843200 | tf_op jit(solution)/shard_map/all_gather | solution.py:407
  11.0 252.9 %all-gather.19.cloned.1.call-start = ((), (), s32[]{:S(2)}) async-start(), calls=%async_computation.14 | async-start | bytes 1843200 | tf_op jit(solution)/shard_map/all_gather | solution.py:407
  11.6 540.4 %reduce-scatter.27.cloned.1.call-start = ((), (), s32[]{:S(2)}) async-start(), calls=%async_computation.17 | async-start | bytes 737280
  12.4 46.4 %copy-start.49 = (bf16[1,288,6,144]{1,3,2,0:T(8,128)(2,1)}, bf16[1,288,6,144]{1,3,2,0:T(8,128)(2,1)S(1)}, u32[]{:S(2)}) copy-start(bf16[1,288,6,144]{1,3,2,0:T(8,128)(2,1)S(1)} %get-tuple-element.179) | copy-start | bytes 1492996
  12.4 46.4 %copy-start.51 = (bf16[1,288,6,144]{1,3,2,0:T(8,128)(2,1)}, bf16[1,288,6,144]{1,3,2,0:T(8,128)(2,1)S(1)}, u32[]{:S(2)}) copy-start(bf16[1,288,6,144]{1,3,2,0:T(8,128)(2,1)S(1)} %get-tuple-element.180) | copy-start | bytes 1492996
  12.4 44.8 %copy-start.69 = (u32[32]{0:T(128)S(1)}, u32[32]{0:T(128)}, u32[]{:S(2)}) copy-start(u32[32]{0:T(128)} %constant.36) | copy-start | bytes 388
  12.4 46.1 %copy-start.61 = (f32[2,6,144]{2,0,1:T(2,128)S(1)}, f32[2,6,144]{2,0,1:T(2,128)}, u32[]{:S(2)}) copy-start(f32[2,6,144]{2,0,1:T(2,128)} %param.16) | copy-start | bytes 20740
  12.4 46.3 %copy-start.55 = (bf16[2,288,3,144]{1,3,2,0:T(8,128)(2,1)S(1)}, bf16[2,288,3,144]{1,3,2,0:T(8,128)(2,1)}, u32[]{:S(2)}) copy-start(bf16[2,288,3,144]{1,3,2,0:T(8,128)(2,1)} %param.17) | copy-start | bytes 1492996
  119.8 36.6 %copy-start.59 = (bf16[256,144]{0,1:T(8,128)(2,1)S(1)}, bf16[256,144]{0,1:T(8,128)(2,1)}, u32[]{:S(2)}) copy-start(bf16[256,144]{0,1:T(8,128)(2,1)} %param.13) | copy-start | bytes 221188
  156.4 33.5 %copy-start.26 = (f32[144,6]{1,0:T(8,128)}, f32[144,6]{1,0:T(8,128)S(1)}, u32[]{:S(2)}) copy-start(f32[144,6]{1,0:T(8,128)S(1)} %get-tuple-element.192.mod_own) | copy-start | bytes 10372
  265.4 42.0 %copy-start.1 = (f32[1152,6]{1,0:T(8,128)S(1)}, f32[1152,6]{1,0:T(8,128)}, u32[]{:S(2)}) copy-start(f32[1152,6]{1,0:T(8,128)} %get-tuple-element.181.mod) | copy-start | bytes 82948
  307.4 50.0 %copy-start.18 = (f32[144,256]{1,0:T(8,128)}, f32[144,256]{1,0:T(8,128)S(1)}, u32[]{:S(2)}) copy-start(f32[144,256]{1,0:T(8,128)S(1)} %get-tuple-element.66) | copy-start | bytes 442372
  307.4 50.7 %copy-start.42 = (bf16[6,72,256]{2,1,0:T(8,128)(2,1)S(1)}, bf16[6,72,256]{2,1,0:T(8,128)(2,1)}, u32[]{:S(2)}) copy-start(bf16[6,72,256]{2,1,0:T(8,128)(2,1)} %copy-done.41) | copy-start | bytes 663556
  307.4 50.7 %copy-start.46 = (f32[144,256]{1,0:T(8,128)S(1)}, f32[144,256]{1,0:T(8,128)}, u32[]{:S(2)}) copy-start(f32[144,256]{1,0:T(8,128)} %copy-done.45) | copy-start | bytes 442372
  307.4 50.7 %copy-start.48 = (f32[1,256]{1,0:T(1,128)S(1)}, f32[1,256]{1,0:T(1,128)}, u32[]{:S(2)}) copy-start(f32[1,256]{1,0:T(1,128)} %copy-done.47) | copy-start | bytes 3076
  358.1 26.4 %copy-start.57 = (bf16[1152,256]{1,0:T(8,128)(2,1)S(1)}, bf16[1152,256]{1,0:T(8,128)(2,1)}, u32[]{:S(2)}) copy-start(bf16[1152,256]{1,0:T(8,128)(2,1)} %get-tuple-element.101) | copy-start | bytes 1769476
  387.6 165.4 %reduce-scatter.25.cloned.1.call-start = ((), (), s32[]{:S(2)}) async-start(), calls=%async_computation.16 | async-start | bytes 737280
  390.6 49.5 %copy-start.28 = (f32[144,6]{1,0:T(8,128)S(1)}, f32[144,6]{1,0:T(8,128)}, u32[]{:S(2)}) copy-start(f32[144,6]{1,0:T(8,128)} %copy-done.26) | copy-start | bytes 10372
  390.6 49.5 %copy-start.40 = (bf16[6,72,256]{2,1,0:T(8,128)(2,1)S(1)}, bf16[6,72,256]{2,1,0:T(8,128)(2,1)}, u32[]{:S(2)}) copy-start(bf16[6,72,256]{2,1,0:T(8,128)(2,1)} %copy-done.39) | copy-start | bytes 663556
  390.6 49.5 %copy-start.44 = (f32[144,256]{1,0:T(8,128)S(1)}, f32[144,256]{1,0:T(8,128)}, u32[]{:S(2)}) copy-start(f32[144,256]{1,0:T(8,128)} %copy-done.43) | copy-start | bytes 442372
  467.8 87.1 %reduce-scatter.19.cloned.1.call-start = ((), (), s32[]{:S(2)}) async-start(), calls=%async_computation.9 | async-start | bytes 1474560 | tf_op jit(solution)/shard_map/reduce_scatter | solution.py:401
  469.4 88.8 %reduce-scatter.17.cloned.1.call-start = ((), (), s32[]{:S(2)}) async-start(), calls=%async_computation.8 | async-start | bytes 1474560 | tf_op jit(solution)/shard_map/reduce_scatter | solution.py:401
  471.0 127.6 %reduce-scatter.31.cloned.1.call-start = ((), (), s32[]{:S(2)}) async-start(), calls=%async_computation.19 | async-start | bytes 2949120
  478.6 153.9 %reduce-scatter.23.cloned.1.call-start = ((), (), s32[]{:S(2)}) async-start(), calls=%async_computation.11 | async-start | bytes 1843200 | tf_op jit(solution)/shard_map/reduce_scatter | solution.py:401
  480.4 185.6 %reduce-scatter.21.cloned.1.call-start = ((), (), s32[]{:S(2)}) async-start(), calls=%async_computation.10 | async-start | bytes 1843200 | tf_op jit(solution)/shard_map/reduce_scatter | solution.py:401
  482.3 41.0 %copy-start.3 = (f32[576,1]{1,0:T(8,128)S(1)}, f32[576,1]{1,0:T(8,128)}, u32[]{:S(2)}) copy-start(f32[576,1]{1,0:T(8,128)} %copy-done.2) | copy-start | bytes 6916
  482.3 41.2 %copy-start.5 = (f32[576,1]{1,0:T(8,128)S(1)}, f32[576,1]{1,0:T(8,128)}, u32[]{:S(2)}) copy-start(f32[576,1]{1,0:T(8,128)} %copy-done.4) | copy-start | bytes 6916
  482.3 224.0 %reduce-scatter.29.cloned.1.call-start = ((), (), s32[]{:S(2)}) async-start(), calls=%async_computation.18 | async-start | bytes 2949120
  483.2 40.5 %copy-start.30 = (bf16[144,256]{1,0:T(8,128)(2,1)S(1)}, bf16[144,256]{1,0:T(8,128)(2,1)}, u32[]{:S(2)}) copy-start(bf16[144,256]{1,0:T(8,128)(2,1)} %copy-done.29) | copy-start | bytes 221188
  668.3 40.4 %copy-start.21 = (f32[144,256]{1,0:T(8,128)S(1)}, f32[144,256]{1,0:T(8,128)}, u32[]{:S(2)}) copy-start(f32[144,256]{1,0:T(8,128)} %copy-done.20) | copy-start | bytes 442372
  (51 other events, 281.5 us)
Sparse Core Ops, SparseCore 0:
  10.4 31.9 all-gather.16
  44.3 35.6 all-gather.20
  81.8 34.3 all-gather.14
  118.5 31.4 all-gather.18
  387.8 26.4 reduce-scatter.26
  467.9 26.6 reduce-scatter.24
  498.0 28.5 reduce-scatter.18
  529.6 28.5 reduce-scatter.16
  561.2 37.3 reduce-scatter.30
  602.0 30.3 reduce-scatter.22
  635.7 30.2 reduce-scatter.20
  668.9 37.3 reduce-scatter.28

commit v2 on v1

v2 whole, which is shorter than its diff:
```python
import functools
import math

import jax
import jax.numpy as jnp
from jax import lax
from jax.experimental import pallas as pl
from jax.experimental.pallas import tpu as pltpu
from jax.sharding import PartitionSpec as P

D = 1152
HEAD = 72
LAYERS = 2
EPS = 1e-06
SCALE = HEAD ** (-0.5)
BF16 = jnp.bfloat16
F32 = jnp.float32
MESH = pl.DeviceIdType.MESH
VMEM_BYTES = 52 * 1024 * 1024


def nn(a, b):
    return lax.dot_general(a, b, (((1,), (0,)), ((), ())), preferred_element_type=F32)


def tn(a, b):
    return lax.dot_general(a, b, (((0,), (0,)), ((), ())), preferred_element_type=F32)


def nt(a, b):
    return lax.dot_general(a, b, (((1,), (1,)), ((), ())), preferred_element_type=F32)


def flat(x):
    blocks, rows, columns = x.shape
    if rows % 16 == 0:
        return x.reshape(blocks * rows, columns)
    return x.astype(F32).reshape(blocks * rows, columns).astype(x.dtype)


class Place:
    def __init__(self, sizes):
        rows, count = sizes
        self.rows = rows
        self.per_row = count // rows
        self.row = lax.axis_index("row")
        self.col = lax.axis_index("col")
        self.count = count
        self.zs = count // 2
        self.z = self.col // 2
        self.core = self.col % 2
        self.mate_core = 1 - self.core
        self.mate = (self.row, self.z * 2 + self.mate_core)

    def ahead(self, k):
        return lax.rem(self.z + k, self.zs)

    def behind(self, k):
        return lax.rem(self.z + self.zs - k, self.zs)

    def peer(self, z):
        return (self.row, z * 2 + self.core)

    def below(self, k):
        return lax.rem(self.row + k, self.rows)

    def above(self, k):
        return lax.rem(self.row + self.rows - k, self.rows)


def greet(here, with_rows=True):
    barrier = pltpu.get_barrier_semaphore()
    pl.semaphore_signal(barrier, inc=1, device_id=here.mate, device_id_type=MESH)
    for k in range(1, here.zs):
        pl.semaphore_signal(
            barrier, inc=1, device_id=here.peer(here.ahead(k)), device_id_type=MESH
        )
    if with_rows:
        for k in range(1, here.rows):
            pl.semaphore_signal(
                barrier, inc=1, device_id=(here.below(k), here.col), device_id_type=MESH
            )
        pl.semaphore_wait(barrier, here.zs + here.rows - 1)
    else:
        pl.semaphore_wait(barrier, here.zs)


def send(src, dst, send_sem, recv_sem, device):
    return pltpu.make_async_remote_copy(
        src_ref=src,
        dst_ref=dst,
        send_sem=send_sem,
        recv_sem=recv_sem,
        device_id=device,
        device_id_type=MESH,
    )


def gather(here, buf, out_sem, fwd_sem, in_sem):
    own = here.col
    started = []
    for k in range(1, here.zs):
        copy = send(
            buf.at[own], buf.at[own], out_sem.at[k], in_sem.at[own], here.peer(here.ahead(k))
        )
        copy.start()
        started.append(copy)
    copy = send(buf.at[own], buf.at[own], out_sem.at[0], in_sem.at[own], here.mate)
    copy.start()
    started.append(copy)
    for k in range(1, here.zs):
        src = here.behind(k) * 2 + here.core
        copy = send(buf.at[src], buf.at[src], fwd_sem.at[k], in_sem.at[src], here.mate)
        copy.wait_recv()
        copy.start()
        started.append(copy)
    for k in range(here.zs):
        src = here.behind(k) * 2 + here.mate_core
        send(buf.at[src], buf.at[src], fwd_sem.at[0], in_sem.at[src], here.mate).wait_recv()
    for copy in started:
        copy.wait_send()


class RowGather:
    def __init__(self, here, src, dst, sems):
        self.here, self.src, self.dst = here, src, dst
        self.out, self.into = sems.at[0], sems.at[1]
        own = here.row
        self.local = pltpu.make_async_copy(src, dst.at[own], self.out.at[0])
        self.local.start()
        self.copies = []
        for k in range(1, here.rows):
            copy = send(
                src, dst.at[own], self.out.at[k], self.into.at[own], (here.below(k), here.col)
            )
            copy.start()
            self.copies.append(copy)

    def finish(self):
        here = self.here
        self.local.wait()
        for k in range(1, here.rows):
            src = here.above(k)
            send(
                self.src, self.dst.at[src], self.out.at[k], self.into.at[src], (src, here.col)
            ).wait_recv()
        for copy in self.copies:
            copy.wait_send()


class RowSum:
    def __init__(self, here, parts, got, sems):
        self.here, self.parts, self.got = here, parts, got
        self.out, self.into = sems.at[0], sems.at[1]
        self.copies = []
        for k in range(1, here.rows):
            to = here.below(k)
            copy = send(
                parts.at[to],
                got.at[here.row],
                self.out.at[k],
                self.into.at[here.row],
                (to, here.col),
            )
            copy.start()
            self.copies.append(copy)

    def finish(self):
        here = self.here
        total = self.parts[here.row].astype(F32)
        for k in range(1, here.rows):
            src = here.above(k)
            send(
                self.parts.at[src],
                self.got.at[src],
                self.out.at[k],
                self.into.at[src],
                (src, here.col),
            ).wait_recv()
            total = total + self.got[src].astype(F32)
        for copy in self.copies:
            copy.wait_send()
        return total


class WeightGrads:
    def __init__(self, here, hidden, grad_in, fed, grad_fed, scratch):
        in_parts, in_got, fed_parts, fed_got, in_sems, fed_sems = scratch
        depth = in_parts.shape[1]
        product = nt(hidden[...], grad_in[...])
        for r in range(here.rows):
            in_parts[r] = product[r * depth : (r + 1) * depth].astype(BF16)
        self.first = RowSum(here, in_parts, in_got, in_sems)
        grad_now = grad_fed[...]
        for r in range(here.rows):
            fed_parts[r] = nt(grad_now, fed[r]).astype(BF16)
        self.second = RowSum(here, fed_parts, fed_got, fed_sems)

    def finish(self, in_out, fed_out):
        in_out[...] = self.first.finish()
        fed_out[...] = self.second.finish()


def scatter_sum(here, parts, near, far, near_sems, far_sems, stat=None, meanwhile=None):
    near_out, near_in = near_sems
    far_out, far_in = far_sems
    z, core = here.z, here.core
    order = list(range(1, here.zs)) + [0]
    near_copies = []
    if stat is not None:
        own, got, sums, others, stat_sems = stat
        stat_out, stat_in = stat_sems
        first = send(own, got, stat_out.at[0], stat_in.at[z], here.mate)
        first.start()
    for k in order:
        to = here.ahead(k)
        copy = send(
            parts.at[here.mate_core, to], near.at[to], near_out.at[k], near_in.at[to], here.mate
        )
        copy.start()
        near_copies.append(copy)
    far_copies = []
    if stat is not None:
        first.wait()
        sums[...] = own[...] + got[...]
        for k in range(1, here.zs):
            copy = send(
                sums, others.at[z], stat_out.at[k], stat_in.at[z], here.peer(here.ahead(k))
            )
            copy.start()
            far_copies.append(copy)
    total = None
    for i, k in enumerate(order):
        to = here.ahead(k)
        near_copies[i].wait_recv()
        both = parts[core, to].astype(F32) + near[to].astype(F32)
        if k == 0:
            total = both
        else:
            parts[core, to] = both.astype(BF16)
            copy = send(
                parts.at[core, to], far.at[z], far_out.at[k], far_in.at[z], here.peer(to)
            )
            copy.start()
            far_copies.append(copy)
    if meanwhile is not None:
        meanwhile()
    stat_total = None
    if stat is not None:
        stat_total = sums[...]
        for k in range(1, here.zs):
            src = here.behind(k)
            send(
                sums, others.at[src], stat_out.at[k], stat_in.at[src], here.peer(src)
            ).wait_recv()
            stat_total = stat_total + others[src]
    for k in range(1, here.zs):
        src = here.behind(k)
        send(
            parts.at[core, src], far.at[src], far_out.at[k], far_in.at[src], here.peer(src)
        ).wait_recv()
        total = total + far[src].astype(F32)
    for copy in near_copies:
        copy.wait_send()
    for copy in far_copies:
        copy.wait_send()
    return total, stat_total


def normalize(stream):
    average = jnp.sum(stream, 0, keepdims=True) / D
    centred = stream - average
    spread = jnp.sum(centred * centred, 0, keepdims=True) / D
    inverse = lax.rsqrt(spread + EPS)
    return centred * inverse, inverse


def gelu(u):
    inner = math.sqrt(2 / math.pi) * (u + 0.044715 * (u * u * u))
    return 0.5 * u * (1.0 + jnp.tanh(inner))


def gelu_slope(u):
    root = math.sqrt(2 / math.pi)
    t = jnp.tanh(root * (u + 0.044715 * (u * u * u)))
    return 0.5 * (1.0 + t) + 0.5 * u * (1.0 - t * t) * (root * (1.0 + 3 * 0.044715 * (u * u)))


def fed_product(here, weight, buf, kept):
    total = 0.0
    for r in range(here.rows):
        piece = flat(buf[r * here.per_row : (r + 1) * here.per_row])
        kept[r] = piece
        total = total + nn(weight[r], piece)
    return total


def attention_forward(
    sizes, stream, mod, mod_own, w_qkv, b_qkv, w_out, b_out, next_in, next_fed,
    normed, inverse, hidden, qkv, log_total, attended, branch, stream_out, all_in, all_fed,
    x_buf, a_buf, x_out, x_fwd, x_in, a_out, a_fwd, a_in, in_sems, fed_sems,
):
    here = Place(sizes)
    greet(here)
    coming = [RowGather(here, next_in, all_in, in_sems), RowGather(here, next_fed, all_fed, fed_sems)]
    x_buf[here.col] = stream[...].astype(BF16)
    gather(here, x_buf, x_out, x_fwd, x_in)
    values, inv = normalize(flat(x_buf[...]).astype(F32))
    normed[...] = values
    inverse[...] = inv
    hidden_now = (values * (1.0 + mod[:, 1:2]) + mod[:, 0:1]).astype(BF16)
    hidden[...] = hidden_now
    projected = tn(flat(w_qkv[...]), hidden_now) + b_qkv[...]
    heads = qkv.shape[0] // 3
    for i in range(3 * heads):
        qkv[i] = projected[i * HEAD : (i + 1) * HEAD].astype(BF16)
    pieces = []
    for h in range(heads):
        scores = tn(qkv[heads + h], qkv[h]) * SCALE
        highest = jnp.max(scores, axis=0, keepdims=True)
        expd = jnp.exp(scores - highest)
        summed = jnp.sum(expd, axis=0, keepdims=True)
        log_total[h] = highest + jnp.log(summed)
        probs = (expd / summed).astype(BF16)
        pieces.append(nn(qkv[2 * heads + h], probs))
    a_buf[here.col] = jnp.concatenate(pieces, axis=0).astype(BF16)
    gather(here, a_buf, a_out, a_fwd, a_in)
    branch_now = b_out[...] + fed_product(here, w_out, a_buf, attended)
    branch[...] = branch_now
    stream_out[...] = stream[...] + mod_own[:, 2:3] * branch_now
    for one in coming:
        one.finish()


def mlp_forward(sizes, more, *refs):
    stream, mod, mod_own, w_one, b_one, w_two, b_two = refs[:7]
    refs = refs[7:]
    if more:
        next_in, next_fed = refs[:2]
        refs = refs[2:]
    normed, inverse, hidden, pre, activated, branch, stream_out = refs[:7]
    refs = refs[7:]
    if more:
        all_in, all_fed = refs[:2]
        refs = refs[2:]
    x_buf, a_buf, x_out, x_fwd, x_in, a_out, a_fwd, a_in = refs[:8]
    here = Place(sizes)
    greet(here, more)
    coming = []
    if more:
        in_sems, fed_sems = refs[8:]
        coming = [RowGather(here, next_in, all_in, in_sems), RowGather(here, next_fed, all_fed, fed_sems)]
    x_buf[here.col] = stream[...].astype(BF16)
    gather(here, x_buf, x_out, x_fwd, x_in)
    values, inv = normalize(flat(x_buf[...]).astype(F32))
    normed[...] = values
    inverse[...] = inv
    hidden_now = (values * (1.0 + mod[:, 4:5]) + mod[:, 3:4]).astype(BF16)
    hidden[...] = hidden_now
    pre_now = tn(flat(w_one[...]), hidden_now) + b_one[...]
    pre[...] = pre_now
    a_buf[here.col] = gelu(pre_now).astype(BF16)
    gather(here, a_buf, a_out, a_fwd, a_in)
    branch_now = b_two[...] + fed_product(here, w_two, a_buf, activated)
    branch[...] = branch_now
    stream_out[...] = stream[...] + mod_own[:, 5:6] * branch_now
    for one in coming:
        one.finish()


def split_parts(here, parts, weight, rows):
    size = parts.shape[2]
    for r in range(here.rows):
        product = tn(weight[r], rows)
        for j in range(here.per_row):
            c = r * here.per_row + j
            parts[c % 2, c // 2] = product[j * size : (j + 1) * size].astype(BF16)


def split_norm_parts(here, parts, stat, weight, rows, normed, gain):
    size = parts.shape[2]
    product = nn(flat(weight[...]), rows)
    for c in range(here.count):
        parts[c % 2, c // 2] = product[c * size : (c + 1) * size].astype(BF16)
    scaled = product * (1.0 + gain)
    stat[...] = jnp.zeros_like(stat)
    stat[0:1] = jnp.sum(scaled, 0, keepdims=True)
    stat[1:2] = jnp.sum(scaled * normed[...], 0, keepdims=True)


def norm_back(here, grad_hidden, totals, normed, inverse, gain):
    width = grad_hidden.shape[0]
    own = normed[pl.ds(pl.multiple_of(here.col * width, 8), width)]
    scaled = grad_hidden * (1.0 + gain)
    change = inverse[...] * (scaled - totals[0:1] / D - own * (totals[1:2] / D))
    shift = jnp.sum(grad_hidden, 1, keepdims=True)
    stretch = jnp.sum(grad_hidden * own, 1, keepdims=True)
    return change, shift, stretch


def mlp_backward(sizes, more, *refs):
    grad, mod, mod_own, branch, pre, normed, inverse, w_one, w_two = refs[:9]
    refs = refs[9:]
    if more:
        feeds = refs[:4]
        refs = refs[4:]
    grad_branch, grad_pre, grad_out, sums, sums_pre = refs[:5]
    refs = refs[5:]
    if more:
        weight_outs = refs[:2]
        refs = refs[2:]
    a_parts, a_near, a_far, h_parts, h_near, h_far, stat_own, stat_got, stat_sum, stat_far = refs[:10]
    an_out, an_in, af_out, af_in, hn_out, hn_in, hf_out, hf_in, st_out, st_in = refs[10:20]
    here = Place(sizes)
    greet(here, more)
    going = []

    def meanwhile():
        if more:
            going.append(WeightGrads(here, *feeds, refs[20:]))

    grad_now = grad[...]
    grad_branch_now = (mod_own[:, 5:6] * grad_now).astype(BF16)
    grad_branch[...] = grad_branch_now
    split_parts(here, a_parts, w_two, grad_branch_now)
    grad_act, _ = scatter_sum(
        here, a_parts, a_near, a_far, (an_out, an_in), (af_out, af_in), None, meanwhile
    )
    grad_pre_now = (grad_act * gelu_slope(pre[...])).astype(BF16)
    grad_pre[...] = grad_pre_now
    split_norm_parts(here, h_parts, stat_own, w_one, grad_pre_now, normed, mod[:, 4:5])
    grad_hidden, totals = scatter_sum(
        here, h_parts, h_near, h_far, (hn_out, hn_in), (hf_out, hf_in),
        (stat_own, stat_got, stat_sum, stat_far, (st_out, st_in)),
    )
    change, shift, stretch = norm_back(
        here, grad_hidden, totals, normed, inverse, mod_own[:, 4:5]
    )
    grad_out[...] = grad_now + change
    sums[:, 0:1] = shift
    sums[:, 1:2] = stretch
    sums[:, 2:3] = jnp.sum(grad_now * branch[...], 1, keepdims=True)
    sums[:, 3:4] = jnp.sum(grad_branch_now.astype(F32), 1, keepdims=True)
    sums_pre[...] = jnp.sum(grad_pre_now.astype(F32), 1, keepdims=True)
    if more:
        going[0].finish(*weight_outs)


def attention_backward(
    sizes, grad, mod, mod_own, branch, qkv, log_total, normed, inverse, w_qkv, w_out,
    feed0, feed1, feed2, feed3,
    grad_branch, grad_qkv, grad_out, sums, sums_qkv, weight_in, weight_fed,
    a_parts, a_near, a_far, h_parts, h_near, h_far, stat_own, stat_got, stat_sum, stat_far,
    an_out, an_in, af_out, af_in, hn_out, hn_in, hf_out, hf_in, st_out, st_in, *row_scratch,
):
    here = Place(sizes)
    greet(here)
    going = []

    def meanwhile():
        going.append(WeightGrads(here, feed0, feed1, feed2, feed3, row_scratch))

    grad_now = grad[...]
    grad_branch_now = (mod_own[:, 2:3] * grad_now).astype(BF16)
    grad_branch[...] = grad_branch_now
    split_parts(here, a_parts, w_out, grad_branch_now)
    grad_att, _ = scatter_sum(
        here, a_parts, a_near, a_far, (an_out, an_in), (af_out, af_in), None, meanwhile
    )
    heads = qkv.shape[0] // 3
    queries, keys, values = [], [], []
    for h in range(heads):
        query, key, value = qkv[h], qkv[heads + h], qkv[2 * heads + h]
        grad_one = grad_att[h * HEAD : (h + 1) * HEAD].astype(BF16)
        weights = jnp.exp(tn(key, query) * SCALE - log_total[h])
        grad_weights = tn(value, grad_one)
        values.append(nt(grad_one, weights.astype(BF16)))
        inner = jnp.sum(weights * grad_weights, axis=0, keepdims=True)
        grad_scores = (weights * (grad_weights - inner)).astype(BF16)
        queries.append(nn(key, grad_scores) * SCALE)
        keys.append(nt(query, grad_scores) * SCALE)
    grad_qkv_now = jnp.concatenate(queries + keys + values, axis=0).astype(BF16)
    grad_qkv[...] = grad_qkv_now
    split_norm_parts(here, h_parts, stat_own, w_qkv, grad_qkv_now, normed, mod[:, 1:2])
    grad_hidden, totals = scatter_sum(
        here, h_parts, h_near, h_far, (hn_out, hn_in), (hf_out, hf_in),
        (stat_own, stat_got, stat_sum, stat_far, (st_out, st_in)),
    )
    change, shift, stretch = norm_back(
        here, grad_hidden, totals, normed, inverse, mod_own[:, 1:2]
    )
    grad_out[...] = grad_now + change
    sums[:, 0:1] = shift
    sums[:, 1:2] = stretch
    sums[:, 2:3] = jnp.sum(grad_now * branch[...], 1, keepdims=True)
    sums[:, 3:4] = jnp.sum(grad_branch_now.astype(F32), 1, keepdims=True)
    sums_qkv[...] = jnp.sum(grad_qkv_now.astype(F32), 1, keepdims=True)
    going[0].finish(weight_in, weight_fed)


def modulation_start(
    sizes, signal, w_mod, b_mod, next_in, next_fed,
    mod_all, signal_part, all_in, all_fed,
    sig_row, sig_col, mod_part, mod_got, mod_col,
    sig_row_sems, s_out, s_fwd, s_in, mod_sems, m_out, m_fwd, m_in, in_sems, fed_sems,
):
    here = Place(sizes)
    greet(here)
    width = signal.shape[1]
    signals = RowGather(here, signal, sig_row, sig_row_sems)
    coming = [RowGather(here, next_in, all_in, in_sems), RowGather(here, next_fed, all_fed, fed_sems)]
    signals.finish()
    sig_col[here.col] = sig_row[...].reshape(here.rows * 8, width)
    gather(here, sig_col, s_out, s_fwd, s_in)
    for j in range(here.per_row):
        signal_part[j] = sig_col[here.row * here.per_row + j]
    for i in range(LAYERS):
        product = 0.0
        for j in range(here.per_row):
            product = product + nn(
                signal_part[j].astype(BF16), w_mod[i, j * width : (j + 1) * width]
            )
        for r in range(here.rows):
            mod_part[r, i] = product[r * 8 : (r + 1) * 8]
    total = RowSum(here, mod_part, mod_got, mod_sems).finish() + b_mod[...]
    mod_col[here.col] = total
    gather(here, mod_col, m_out, m_fwd, m_in)
    mod_all[...] = mod_col[...]
    for one in coming:
        one.finish()


def modulation_end(
    sizes, grad_mod, biases, w_mod, feed0, feed1, feed2, feed3,
    mod_all, bias_sum, grad_signal, weight_in, weight_fed,
    mod_row, bias_row, back_col, back_own, back_row,
    mod_sems, bias_sems, b_out, b_fwd, b_in, back_sems, *row_scratch,
):
    here = Place(sizes)
    greet(here)
    mods = RowGather(here, grad_mod, mod_row, mod_sems)
    shares = RowGather(here, biases, bias_row, bias_sems)
    going = WeightGrads(here, feed0, feed1, feed2, feed3, row_scratch)
    mods.finish()
    mod_all[...] = mod_row[...]
    product = 0.0
    for i in range(LAYERS):
        rows = mod_row[:, i].reshape(here.rows * 8, mod_row.shape[3])
        product = product + nt(rows.astype(BF16), w_mod[i])
    back_col[here.col] = product
    gather(here, back_col, b_out, b_fwd, b_in)
    back_own[...] = jnp.sum(back_col[...], axis=0)
    backs = RowGather(here, back_own, back_row, back_sems)
    shares.finish()
    bias_sum[...] = jnp.sum(bias_row[...], axis=0)
    backs.finish()
    grad_signal[...] = back_row[
        here.col // here.per_row, pl.ds(pl.multiple_of(here.row * 8, 8), 8)
    ]
    going.finish(weight_in, weight_fed)


def run(body, ident, args, outs, scratch, far_args=0, far_outs=0):
    vmem = pl.BlockSpec(memory_space=pltpu.VMEM)
    anywhere = pl.BlockSpec(memory_space=pl.ANY)
    return pl.pallas_call(
        body,
        out_shape=[jax.ShapeDtypeStruct(shape, dtype) for shape, dtype in outs],
        in_specs=[vmem] * (len(args) - far_args) + [anywhere] * far_args,
        out_specs=[vmem] * (len(outs) - far_outs) + [anywhere] * far_outs,
        scratch_shapes=scratch,
        compiler_params=pltpu.CompilerParams(
            collective_id=ident, has_side_effects=True, vmem_limit_bytes=VMEM_BYTES
        ),
    )(*args)


def dma(*shape):
    return pltpu.SemaphoreType.DMA(shape)


def gather_scratch(count, sizes, width):
    bufs = [pltpu.VMEM((count, size, width), BF16) for size in sizes]
    return bufs + [dma(count) for _ in range(3 * len(sizes))]


def scatter_scratch(count, sizes, width):
    zs = count // 2
    bufs = []
    for size in sizes:
        bufs.append(pltpu.VMEM((2, zs, size, width), BF16))
        bufs.append(pltpu.VMEM((zs, size, width), BF16))
        bufs.append(pltpu.VMEM((zs, size, width), BF16))
    bufs += [pltpu.VMEM((8, width), F32) for _ in range(3)]
    bufs.append(pltpu.VMEM((zs, 8, width), F32))
    return bufs + [dma(zs) for _ in range(4 * len(sizes) + 2)]


def per_device(
    sizes,
    tokens, cond, w_mod, b_mod, query_key_value_weight, b_qv,
    attention_output_weight, attention_output_bias, first_linear_weight, first_linear_bias,
    second_linear_weight, second_linear_bias, cotangent,
):
    rows, count = sizes
    assert cond.shape[0] == 1
    length, width = tokens.shape
    heads = width // HEAD
    hidden_width = first_linear_weight.shape[2]
    rows_in = w_mod.shape[1]
    rows_fed = second_linear_weight.shape[1]
    per_row = count // rows
    cond_float = cond.astype(F32)
    signal = jax.nn.silu(cond_float).astype(BF16).astype(F32)
    w_mod_flat = w_mod.reshape(LAYERS, rows_in, 6 * width)

    shards = []
    for i in range(LAYERS):
        shards.append(
            (
                query_key_value_weight[i].reshape(rows_in, 3 * width),
                attention_output_weight[i].T,
                first_linear_weight[i],
                second_linear_weight[i].T,
            )
        )

    def gathered(first):
        if first:
            return [((rows, rows_in, 3 * width), BF16), ((rows, width, rows_in), BF16)]
        return [((rows, rows_in, hidden_width), BF16), ((rows, width, rows_fed), BF16)]

    def grads(first):
        return [(shape[1:], F32) for shape, _ in gathered(first)]

    def grad_scratch(first):
        (one, _), (two, _) = gathered(first)
        return [
            pltpu.VMEM(one, BF16),
            pltpu.VMEM(one, BF16),
            pltpu.VMEM(two, BF16),
            pltpu.VMEM(two, BF16),
            dma(2, rows),
            dma(2, rows),
        ]

    mod_all, signal_part, w_qkv, w_out = run(
        functools.partial(modulation_start, sizes), 0,
        (
            jnp.broadcast_to(signal, (8, width)),
            w_mod_flat,
            b_mod.reshape(LAYERS, 1, 6 * width),
            shards[0][0],
            shards[0][1],
        ),
        [
            ((count, LAYERS, 8, 6 * width), F32),
            ((per_row, rows * 8, width), F32),
        ]
        + gathered(True),
        [
            pltpu.VMEM((rows, 8, width), F32),
            pltpu.VMEM((count, rows * 8, width), F32),
            pltpu.VMEM((rows, LAYERS, 8, 6 * width), F32),
            pltpu.VMEM((rows, LAYERS, 8, 6 * width), F32),
            pltpu.VMEM((count, LAYERS, 8, 6 * width), F32),
            dma(2, rows), dma(count), dma(count), dma(count),
            dma(2, rows), dma(count), dma(count), dma(count),
            dma(2, rows), dma(2, rows),
        ],
        2, 2,
    )
    mods = mod_all[:, :, 0].reshape(count, LAYERS, 6, width).transpose(1, 0, 3, 2)
    mod_full = mods.reshape(LAYERS, D, 6)
    mod_own = lax.dynamic_index_in_dim(mods, lax.axis_index("col"), 1, keepdims=False)

    stream = tokens.astype(F32).T
    saved = []
    for i in range(LAYERS):
        bias = jnp.concatenate([b_qv[i, 0], jnp.zeros_like(b_qv[i, 0]), b_qv[i, 1]])[:, None]
        normed1, inverse1, hidden1, qkv, log_total, attended, branch1, stream, w_one, w_two = run(
            functools.partial(attention_forward, sizes), 1,
            (
                stream, mod_full[i], mod_own[i], w_qkv, bias, w_out,
                attention_output_bias[i][:, None], shards[i][2], shards[i][3],
            ),
            [
                ((D, length), F32),
                ((1, length), F32),
                ((D, length), BF16),
                ((3 * heads, HEAD, length), BF16),
                ((heads, 1, length), F32),
                ((rows, rows_in, length), BF16),
                ((width, length), F32),
                ((width, length), F32),
            ]
            + gathered(False),
            gather_scratch(count, (width, width), length) + [dma(2, rows), dma(2, rows)],
            2, 2,
        )
        more = i + 1 < LAYERS
        results = run(
            functools.partial(mlp_forward, sizes, more), 2 if more else 3,
            (
                stream, mod_full[i], mod_own[i], w_one, first_linear_bias[i][:, None], w_two,
                second_linear_bias[i][:, None],
            )
            + (shards[i + 1][:2] if more else ()),
            [
                ((D, length), F32),
                ((1, length), F32),
                ((D, length), BF16),
                ((hidden_width, length), F32),
                ((rows, rows_fed, length), BF16),
                ((width, length), F32),
                ((width, length), F32),
            ]
            + (gathered(True) if more else []),
            gather_scratch(count, (width, hidden_width), length)
            + ([dma(2, rows), dma(2, rows)] if more else []),
            2 if more else 0, 2 if more else 0,
        )
        normed2, inverse2, hidden2, pre, activated, branch2, stream = results[:7]
        saved.append(
            (
                normed1, inverse1, hidden1, qkv, log_total, attended, branch1,
                normed2, inverse2, hidden2, pre, activated, branch2,
                w_qkv, w_out, w_one, w_two,
            )
        )
        if more:
            w_qkv, w_out = results[7:]
    output = stream.T.astype(BF16)

    grad = cotangent.astype(F32).T
    grad_mods = [None] * LAYERS
    biases = [None] * LAYERS
    first_grads = [None] * LAYERS
    second_grads = [None] * LAYERS
    waiting = None
    for i in reversed(range(LAYERS)):
        (
            normed1, inverse1, hidden1, qkv, log_total, attended, branch1,
            normed2, inverse2, hidden2, pre, activated, branch2,
            w_qkv, w_out, w_one, w_two,
        ) = saved[i]
        more = waiting is not None
        results = run(
            functools.partial(mlp_backward, sizes, more), 6 if more else 4,
            (grad, mod_full[i], mod_own[i], branch2, pre, normed2, inverse2, w_one, w_two)
            + (waiting if more else ()),
            [
                ((width, length), BF16),
                ((hidden_width, length), BF16),
                ((width, length), F32),
                ((width, 4), F32),
                ((hidden_width, 1), F32),
            ]
            + (grads(True) if more else []),
            scatter_scratch(count, (hidden_width, width), length)
            + (grad_scratch(True) if more else []),
        )
        grad_branch2, grad_pre, grad, sums2, sums_pre = results[:5]
        if more:
            first_grads[i + 1] = results[5:]
        grad_branch1, grad_qkv, grad, sums1, sums_qkv, *second_grads[i] = run(
            functools.partial(attention_backward, sizes), 5,
            (
                grad, mod_full[i], mod_own[i], branch1, qkv, log_total, normed1, inverse1,
                w_qkv, w_out, hidden2, grad_pre, activated, grad_branch2,
            ),
            [
                ((width, length), BF16),
                ((3 * width, length), BF16),
                ((width, length), F32),
                ((width, 4), F32),
                ((3 * width, 1), F32),
            ]
            + grads(False),
            scatter_scratch(count, (width, width), length) + grad_scratch(False),
        )
        waiting = (hidden1, grad_qkv, attended, grad_branch1)
        grad_mods[i] = jnp.concatenate([sums1[:, 0:3], sums2[:, 0:3]], axis=1).T.astype(BF16)
        biases[i] = jnp.concatenate(
            [sums_qkv[:width, 0], sums_qkv[2 * width :, 0], sums1[:, 3], sums2[:, 3], sums_pre[:, 0]]
        )
    mod_grad = jnp.stack(grad_mods).reshape(LAYERS, 1, 6 * width).astype(F32)
    bias_grad = jnp.stack(biases).reshape(1, -1)
    mod_grad_all, bias_sum, grad_signal, *first_grads[0] = run(
        functools.partial(modulation_end, sizes), 7,
        (
            jnp.broadcast_to(mod_grad, (LAYERS, 8, 6 * width)),
            jnp.broadcast_to(bias_grad, (8, bias_grad.shape[1])),
            w_mod_flat,
        )
        + waiting,
        [
            ((rows, LAYERS, 8, 6 * width), F32),
            ((8, bias_grad.shape[1]), F32),
            ((8, rows_in), F32),
        ]
        + grads(True),
        [
            pltpu.VMEM((rows, LAYERS, 8, 6 * width), F32),
            pltpu.VMEM((rows, 8, bias_grad.shape[1]), F32),
            pltpu.VMEM((count, rows * 8, rows_in), F32),
            pltpu.VMEM((rows * 8, rows_in), F32),
            pltpu.VMEM((rows, rows * 8, rows_in), F32),
            dma(2, rows), dma(2, rows), dma(count), dma(count), dma(count), dma(2, rows),
        ]
        + grad_scratch(True),
    )
    signals = signal_part.reshape(per_row, rows, 8, width)[:, :, 0]
    signals = signals.transpose(1, 0, 2).reshape(rows, rows_in)
    mod_rows = mod_grad_all[:, :, 0]
    grad_w_mod = jnp.einsum(
        "ri,rlj->lij",
        signals.astype(BF16),
        mod_rows.astype(BF16),
        preferred_element_type=F32,
    ).reshape(LAYERS, rows_in, 6, width)
    grad_b_mod = jnp.sum(mod_rows, 0).reshape(LAYERS, 6, width)
    grad_signal = lax.dynamic_slice(
        grad_signal[:1], (0, lax.axis_index("col") % per_row * width), (1, width)
    )
    grad_cond = jax.vjp(jax.nn.silu, cond_float)[1](grad_signal)[0]
    bias_sum = bias_sum[0].reshape(LAYERS, -1)
    return (
        output,
        grad.T,
        grad_cond,
        grad_w_mod,
        grad_b_mod,
        jnp.stack([one[0] for one in first_grads]).reshape(LAYERS, rows_in, 3, width),
        bias_sum[:, : 2 * width].reshape(LAYERS, 2, width),
        jnp.stack([one[1].T for one in first_grads]),
        bias_sum[:, 2 * width : 3 * width],
        jnp.stack([one[0] for one in second_grads]),
        bias_sum[:, 4 * width :],
        jnp.stack([one[1].T for one in second_grads]),
        bias_sum[:, 3 * width : 4 * width],
    )


def solution(mesh):
    in_specs = (
        P("row", "col"),
        P("row", "col"),
        P(None, "row", None, "col"),
        P(None, None, "col"),
        P(None, "row", None, "col"),
        P(None, None, "col"),
        P(None, "row", "col"),
        P(None, "col"),
        P(None, "row", "col"),
        P(None, "col"),
        P(None, "row", "col"),
        P(None, "col"),
        P("row", "col"),
    )
    out_specs = (
        P("row", "col"),
        P("row", "col"),
        P("row", "col"),
        P(None, "row", None, "col"),
        P(None, None, "col"),
        P(None, "row", None, "col"),
        P(None, None, "col"),
        P(None, "row", "col"),
        P(None, "col"),
        P(None, "row", "col"),
        P(None, "col"),
        P(None, "row", "col"),
        P(None, "col"),
    )
    return jax.shard_map(
        functools.partial(per_device, (mesh.shape["row"], mesh.shape["col"])),
        mesh=mesh,
        in_specs=in_specs,
        out_specs=out_specs,
        check_vma=False,
    )
```

time: 717 us -> 440 us (0.61)
  blocking collectives: 189 us -> 0 us
  waiting for transfers between devices: 146 us -> 0 us
  Pallas kernels: 282 us -> 409 us
  local copies, waits for them, and re-layouts: 55.2 us -> 19 us
  between operations: 15.9 us -> 1.3 us
  matrix products: 16 us -> 1.82 us
    pallas_call x8 -> x10, Pallas kernels: 282 us -> 409 us  [run(): pl.pallas_call(body, out_shape=[jax.ShapeDtypeStruct(shape, dtype) for sh...]
    all_gather x9 -> x0, blocking collectives: 126 us -> none  [the longest x4 76.8 us: whole_rows(): full = lax.all_gather(weight, 'row', axis=0, tiled=True)]
    unnamed x16 -> x0, waiting for transfers between devices: 77.5 us -> none
    reduce_scatter x4 -> x0, waiting for transfers between devices: 68.1 us -> none  [weight_grad(): lax.psum_scatter(product.astype(BF16), 'row', scatter_dimension=0, tiled=...]
    unnamed x2 -> x0, blocking collectives: 33.6 us -> none
    unnamed x170 -> x49, local copies, waits for them, and re-layouts: 38.2 us -> 5.18 us
    psum x2 -> x0, blocking collectives: 29.9 us -> none  [the longest x1 15.3 us: per_device(): bias_sums = lax.psum([results[i][6] for i in range(LAYERS)], 'row')]
    dot_general x14 -> x1, matrix products: 16 us -> 1.82 us  [per_device(): jnp.einsum('ri,rlj->lij', signals.astype(BF16), mod_rows.astype(BF16), pr...]
  transfers between devices with their start and end apart: 12 -> 0, of which waited for: 5 -> 0; matrix products, arithmetic and copies ran while one was open for 8% -> 0% of each run, Pallas kernels for 23% -> 0%
where the time goes in v2:
time: 440 us; the launch traced here: 439 us
  Pallas kernels  409 us (93%)
  local copies, waits for them, and re-layouts  19 us (4%)
  other arithmetic  7.87 us (2%)
    pallas_call x10, Pallas kernels, run(): pl.pallas_call(body, out_shape=[jax.ShapeDtypeStruct(shape, dtype) for sh...  409 us

profile of v2, /device:TPU:0, one launch (start us, length us, event | category | flops | bytes accessed | tf_op | source)
XLA Modules:
  0.0 439.4 jit_solution(9230078396803648430)
XLA Ops:
  0.7 1.0 convert_bitcast_fusion.1.stream
  1.6 0.7 convert_convert_fusion
  2.3 2.4 copy.63.w_mod
  5.1 0.6 copy-done.12
  5.7 34.8 %shard_map.228 = (f32[8,2,8,864]{3,2,1,0:T(8,128)S(1)}, f32[2,32,144]{2,1,0:T(8,128)S(1)}, bf16[4,288,432]{2,1,0:T(8,128)(2,1)}, bf16[4,144,288]{2,1,0:T(8,128)(2,1)S(1)}) custom-call(f32[8,144]{1,0:T(8,128)S(1)} %broadcast_in_dim.30.signal, bf16[2,288,864]{2,1,0:T(8,128)(2,1)} %copy.63.w_mod, f32[2,1,864]{2,1,0:T(1,128)S(1)} %reshape.97.b_mod, ...), custom_call_target="tpu_custom_call" | custom-call | tf_op jit(solution)/shard_map/pallas_call | solution.py:566
  40.5 0.8 copy-done.1
  41.4 1.1 copy.67
  43.7 39.4 %shard_map.229 = (f32[1152,256]{1,0:T(8,128)}, f32[1,256]{1,0:T(1,128)S(1)}, bf16[1152,256]{1,0:T(8,128)(2,1)}, bf16[6,72,256]{2,1,0:T(8,128)(2,1)S(1)}, f32[2,1...) custom-call(f32[144,256]{1,0:T(8,128)S(1)} %convert_bitcast_fusion.1, ...), custom_call_target="tpu_custom_call" | custom-call | tf_op jit(solution)/shard_map/pallas_call | solution.py:566
  83.6 40.2 %shard_map.230 = (f32[1152,256]{1,0:T(8,128)}, f32[1,256]{1,0:T(1,128)S(1)}, bf16[1152,256]{1,0:T(8,128)(2,1)}, f32[576,256]{1,0:T(8,128)}, bf16[4,1152,256]{2,1...) custom-call(f32[144,256]{1,0:T(8,128)S(1)} %get-tuple-element.87.ref, ...), custom_call_target="tpu_custom_call" | custom-call | tf_op jit(solution)/shard_map/pallas_call | solution.py:566
  123.8 0.8 copy-done.2
  124.5 1.1 copy.74
  125.9 44.9 %shard_map.231 = (f32[1152,256]{1,0:T(8,128)}, f32[1,256]{1,0:T(1,128)S(1)}, bf16[1152,256]{1,0:T(8,128)(2,1)}, bf16[6,72,256]{2,1,0:T(8,128)(2,1)S(1)}, f32[2,1...) custom-call(f32[144,256]{1,0:T(8,128)S(1)} %get-tuple-element.90.str, ...), custom_call_target="tpu_custom_call" | custom-call | tf_op jit(solution)/shard_map/pallas_call | solution.py:566
  171.1 38.6 %shard_map.232 = (f32[1152,256]{1,0:T(8,128)}, f32[1,256]{1,0:T(1,128)S(1)}, bf16[1152,256]{1,0:T(8,128)(2,1)S(1)}, f32[576,256]{1,0:T(8,128)}, bf16[4,1152,256]...) custom-call(f32[144,256]{1,0:T(8,128)S(1)} %get-tuple-element.93.refs_0_, f32[1152,6]{1,0:T(8,128)} %bitcast.96, ...), custom_call_target="tpu_custom_call" | custom-call | tf_op jit(solution)/shard_map/pallas_call | solution.py:566
  209.7 0.8 copy-done.3
  210.6 0.6 convert_bitcast_fusion.2
  211.2 50.2 %shard_map.233 = (bf16[144,256]{1,0:T(8,128)(2,1)S(1)}, bf16[576,256]{1,0:T(8,128)(2,1)S(1)}, f32[144,256]{1,0:T(8,128)S(1)}, f32[144,4]{1,0:T(8,128)S(1)}, f32[576,1]{1,0:T(8,128)S(1)}) custom-call(f32[144,256]{1,0:T(8,128)S(1)} %convert_bitcast_fusion.refs_0_, f32[1152,6]{1,0:T(8,128)S(1)} %bitcast.98, f32[144,6]{1,0:T(8,128)S(1)} %get-tuple-element.208.mod_own.refs_2_, ...), custom_call_target="tpu_custom_call" | custom-call | tf_op jit(solution)/shard_map/pallas_call | solution.py:566
  261.4 42.1 %shard_map.234 = (bf16[144,256]{1,0:T(8,128)(2,1)S(1)}, bf16[432,256]{1,0:T(8,128)(2,1)S(1)}, f32[144,256]{1,0:T(8,128)S(1)}, f32[144,4]{1,0:T(8,128)S(1)}, f32[...) custom-call(f32[144,256]{1,0:T(8,128)S(1)} %get-tuple-element.101.grad, f32[1152,6]{1,0:T(8,128)} %bitcast.97, ...), custom_call_target="tpu_custom_call" | custom-call | tf_op jit(solution)/shard_map/pallas_call | solution.py:566
  303.5 46.2 %shard_map.235 = (bf16[144,256]{1,0:T(8,128)(2,1)S(1)}, bf16[576,256]{1,0:T(8,128)(2,1)S(1)}, f32[144,256]{1,0:T(8,128)S(1)}, f32[144,4]{1,0:T(8,128)S(1)}, f32[...) custom-call(f32[144,256]{1,0:T(8,128)S(1)} %get-tuple-element.111.refs_0_, f32[1152,6]{1,0:T(8,128)} %bitcast.104, ...), custom_call_target="tpu_custom_call" | custom-call | tf_op jit(solution)/shard_map/pallas_call | solution.py:566
  349.8 41.2 %shard_map.236 = (bf16[144,256]{1,0:T(8,128)(2,1)S(1)}, bf16[432,256]{1,0:T(8,128)(2,1)S(1)}, f32[144,256]{1,0:T(8,128)S(1)}, f32[144,4]{1,0:T(8,128)S(1)}, f32[...) custom-call(f32[144,256]{1,0:T(8,128)S(1)} %get-tuple-element.120.grad, f32[1152,6]{1,0:T(8,128)} %bitcast.105, ...), custom_call_target="tpu_custom_call" | custom-call | tf_op jit(solution)/shard_map/pallas_call | solution.py:566
  393.4 31.9 %shard_map.237 = (f32[4,2,8,864]{3,2,1,0:T(8,128)S(1)}, f32[8,2304]{1,0:T(8,128)S(1)}, f32[8,288]{1,0:T(8,128)S(1)}, f32[288,432]{1,0:T(8,128)S(1)}, f32[144,288]{1,0:T(8,128)S(1)}) custom-call(f32[2,8,864]{2,1,0:T(8,128)S(1)} %broadcast_in_dim.33.grad_mod, f32[8,2304]{1,0:T(8,128)S(1)} %broadcast_in_dim.35.biases, bf16[2,288,864]{2,1,0:T(8,128)(2,1)} %copy.63.w_mod, ...), custom_call_target="tpu_custom_call" | custom-call | tf_op jit(solution)/shard_map/pallas_call | solution.py:566
  425.3 0.6 fusion.5
  426.1 1.8 convolution_bitcast_fusion
  427.9 3.2 copy.87
  431.2 0.6 copy.90
  432.3 1.2 pad_maximum_fusion.1
  433.6 0.7 reshape.94
  434.3 0.8 pad_maximum_fusion.3
  435.1 0.7 fusion.8
  435.7 1.2 pad_maximum_fusion
  436.9 0.7 slice.204
  437.6 1.1 pad_maximum_fusion.2
  438.8 0.7 copy.105
  (108 shorter events, 5.6 us)
Async XLA Ops:
  0.6 4.1 copy-start.14
  0.7 4.2 copy-start.7
  4.7 0.9 copy-start.12
  5.7 37.0 %copy-start.16 = (f32[2,2,144]{2,1,0:T(2,128)S(1)}, f32[2,2,144]{2,1,0:T(2,128)}, u32[]{:S(2)}) copy-start(f32[2,2,144]{2,1,0:T(2,128)} %param.18) | copy-start | bytes 6916
  40.5 0.8 copy-start.1
  41.3 1.7 copy-start.18
  41.3 1.8 copy-start.4
  42.5 1.1 copy-start.8
  43.7 39.4 %copy-start.15 = (f32[2,576]{1,0:T(2,128)S(1)}, f32[2,576]{1,0:T(2,128)}, u32[]{:S(2)}) copy-start(f32[2,576]{1,0:T(2,128)} %param.22) | copy-start | bytes 13828
  43.7 39.6 %copy-start.19 = (f32[2,144]{1,0:T(2,128)S(1)}, f32[2,144]{1,0:T(2,128)}, u32[]{:S(2)}) copy-start(f32[2,144]{1,0:T(2,128)} %param.24) | copy-start | bytes 3460
  123.8 0.8 copy-start.2
  171.1 40.1 %copy-start.13 = (bf16[256,144]{0,1:T(8,128)(2,1)S(1)}, bf16[256,144]{0,1:T(8,128)(2,1)}, u32[]{:S(2)}) copy-start(bf16[256,144]{0,1:T(8,128)(2,1)} %param.25) | copy-start | bytes 221188
  171.1 40.1 %copy-start = (f32[1,8,144,6]{3,2,1,0:T(8,128)S(1)}, f32[1,8,144,6]{3,2,1,0:T(8,128)}, u32[]{:S(2)}) copy-start(f32[1,8,144,6]{3,2,1,0:T(8,128)} %copy.74) | copy-start | bytes 82948
  209.7 0.8 copy-start.3
  393.3 31.9 %copy-start.17 = (bf16[1,144]{1,0:T(2,128)(2,1)S(1)}, bf16[1,144]{1,0:T(2,128)(2,1)}, u32[]{:S(2)}) copy-start(bf16[1,144]{1,0:T(2,128)(2,1)} %param.14) | copy-start | bytes 868
  427.9 3.9 copy-start.11
  432.3 3.4 copy-start.5
  433.5 2.2 copy-start.6
  435.7 1.9 copy-start.9
  435.7 1.9 copy-start.10

commit v3 on v2

--- a/solution.py
+++ b/solution.py
@@ -183,22 +183,21 @@
         return total
 
 
-class WeightGrads:
-    def __init__(self, here, hidden, grad_in, fed, grad_fed, scratch):
-        in_parts, in_got, fed_parts, fed_got, in_sems, fed_sems = scratch
-        depth = in_parts.shape[1]
-        product = nt(hidden[...], grad_in[...])
-        for r in range(here.rows):
-            in_parts[r] = product[r * depth : (r + 1) * depth].astype(BF16)
-        self.first = RowSum(here, in_parts, in_got, in_sems)
-        grad_now = grad_fed[...]
-        for r in range(here.rows):
-            fed_parts[r] = nt(grad_now, fed[r]).astype(BF16)
-        self.second = RowSum(here, fed_parts, fed_got, fed_sems)
-
-    def finish(self, in_out, fed_out):
-        in_out[...] = self.first.finish()
-        fed_out[...] = self.second.finish()
+def in_grad(here, hidden, grad, scratch):
+    parts, got, sems = scratch
+    depth = parts.shape[1]
+    product = nt(hidden[...], grad[...])
+    for r in range(here.rows):
+        parts[r] = product[r * depth : (r + 1) * depth].astype(BF16)
+    return RowSum(here, parts, got, sems)
+
+
+def fed_grad(here, fed, grad, scratch):
+    parts, got, sems = scratch
+    grad_now = grad[...]
+    for r in range(here.rows):
+        parts[r] = nt(grad_now, fed[r]).astype(BF16)
+    return RowSum(here, parts, got, sems)
 
 
 def scatter_sum(here, parts, near, far, near_sems, far_sems, stat=None, meanwhile=None):
@@ -296,13 +295,14 @@
 
 
 def attention_forward(
-    sizes, stream, mod, mod_own, w_qkv, b_qkv, w_out, b_out, next_in, next_fed,
-    normed, inverse, hidden, qkv, log_total, attended, branch, stream_out, all_in, all_fed,
-    x_buf, a_buf, x_out, x_fwd, x_in, a_out, a_fwd, a_in, in_sems, fed_sems,
+    sizes, stream, mod, mod_own, w_qkv, b_qkv, b_out, fed, next_in,
+    normed, inverse, hidden, qkv, log_total, attended, branch, stream_out, w_out, all_in,
+    x_buf, a_buf, x_out, x_fwd, x_in, a_out, a_fwd, a_in, w_buf, fed_sems, in_sems,
 ):
     here = Place(sizes)
     greet(here)
-    coming = [RowGather(here, next_in, all_in, in_sems), RowGather(here, next_fed, all_fed, fed_sems)]
+    needed = RowGather(here, fed, w_buf, fed_sems)
+    coming = RowGather(here, next_in, all_in, in_sems)
     x_buf[here.col] = stream[...].astype(BF16)
     gather(here, x_buf, x_out, x_fwd, x_in)
     values, inv = normalize(flat(x_buf[...]).astype(F32))
@@ -325,31 +325,31 @@
         pieces.append(nn(qkv[2 * heads + h], probs))
     a_buf[here.col] = jnp.concatenate(pieces, axis=0).astype(BF16)
     gather(here, a_buf, a_out, a_fwd, a_in)
-    branch_now = b_out[...] + fed_product(here, w_out, a_buf, attended)
+    needed.finish()
+    w_out[...] = w_buf[...]
+    branch_now = b_out[...] + fed_product(here, w_buf, a_buf, attended)
     branch[...] = branch_now
     stream_out[...] = stream[...] + mod_own[:, 2:3] * branch_now
-    for one in coming:
-        one.finish()
+    coming.finish()
 
 
 def mlp_forward(sizes, more, *refs):
-    stream, mod, mod_own, w_one, b_one, w_two, b_two = refs[:7]
+    stream, mod, mod_own, w_one, b_one, b_two, fed = refs[:7]
     refs = refs[7:]
     if more:
-        next_in, next_fed = refs[:2]
-        refs = refs[2:]
-    normed, inverse, hidden, pre, activated, branch, stream_out = refs[:7]
-    refs = refs[7:]
+        next_in = refs[0]
+        refs = refs[1:]
+    normed, inverse, hidden, pre, activated, branch, stream_out, w_two = refs[:8]
+    refs = refs[8:]
     if more:
-        all_in, all_fed = refs[:2]
-        refs = refs[2:]
-    x_buf, a_buf, x_out, x_fwd, x_in, a_out, a_fwd, a_in = refs[:8]
+        all_in = refs[0]
+        refs = refs[1:]
+    x_buf, a_buf, x_out, x_fwd, x_in, a_out, a_fwd, a_in, w_buf, fed_sems = refs[:10]
     here = Place(sizes)
-    greet(here, more)
-    coming = []
+    greet(here)
+    needed = RowGather(here, fed, w_buf, fed_sems)
     if more:
-        in_sems, fed_sems = refs[8:]
-        coming = [RowGather(here, next_in, all_in, in_sems), RowGather(here, next_fed, all_fed, fed_sems)]
+        coming = RowGather(here, next_in, all_in, refs[10])
     x_buf[here.col] = stream[...].astype(BF16)
     gather(here, x_buf, x_out, x_fwd, x_in)
     values, inv = normalize(flat(x_buf[...]).astype(F32))
@@ -361,11 +361,13 @@
     pre[...] = pre_now
     a_buf[here.col] = gelu(pre_now).astype(BF16)
     gather(here, a_buf, a_out, a_fwd, a_in)
-    branch_now = b_two[...] + fed_product(here, w_two, a_buf, activated)
+    needed.finish()
+    w_two[...] = w_buf[...]
+    branch_now = b_two[...] + fed_product(here, w_buf, a_buf, activated)
     branch[...] = branch_now
     stream_out[...] = stream[...] + mod_own[:, 5:6] * branch_now
-    for one in coming:
-        one.finish()
+    if more:
+        coming.finish()
 
 
 def split_parts(here, parts, weight, rows):
@@ -399,25 +401,26 @@
 
 
 def mlp_backward(sizes, more, *refs):
-    grad, mod, mod_own, branch, pre, normed, inverse, w_one, w_two = refs[:9]
-    refs = refs[9:]
+    grad, mod, mod_own, branch, pre, normed, inverse, w_one, w_two, activated = refs[:10]
+    refs = refs[10:]
     if more:
-        feeds = refs[:4]
-        refs = refs[4:]
-    grad_branch, grad_pre, grad_out, sums, sums_pre = refs[:5]
-    refs = refs[5:]
+        feeds = refs[:2]
+        refs = refs[2:]
+    grad_branch, grad_pre, grad_out, sums, sums_pre, weight_fed = refs[:6]
+    refs = refs[6:]
     if more:
-        weight_outs = refs[:2]
-        refs = refs[2:]
+        weight_in = refs[0]
+        refs = refs[1:]
     a_parts, a_near, a_far, h_parts, h_near, h_far, stat_own, stat_got, stat_sum, stat_far = refs[:10]
     an_out, an_in, af_out, af_in, hn_out, hn_in, hf_out, hf_in, st_out, st_in = refs[10:20]
     here = Place(sizes)
-    greet(here, more)
+    greet(here)
     going = []
 
     def meanwhile():
+        going.append(fed_grad(here, activated, grad_branch, refs[20:23]))
         if more:
-            going.append(WeightGrads(here, *feeds, refs[20:]))
+            going.append(in_grad(here, *feeds, refs[23:26]))
 
     grad_now = grad[...]
     grad_branch_now = (mod_own[:, 5:6] * grad_now).astype(BF16)
@@ -442,14 +445,15 @@
     sums[:, 2:3] = jnp.sum(grad_now * branch[...], 1, keepdims=True)
     sums[:, 3:4] = jnp.sum(grad_branch_now.astype(F32), 1, keepdims=True)
     sums_pre[...] = jnp.sum(grad_pre_now.astype(F32), 1, keepdims=True)
+    weight_fed[...] = going[0].finish()
     if more:
-        going[0].finish(*weight_outs)
+        weight_in[...] = going[1].finish()
 
 
 def attention_backward(
     sizes, grad, mod, mod_own, branch, qkv, log_total, normed, inverse, w_qkv, w_out,
-    feed0, feed1, feed2, feed3,
-    grad_branch, grad_qkv, grad_out, sums, sums_qkv, weight_in, weight_fed,
+    attended, hidden_two, grad_pre,
+    grad_branch, grad_qkv, grad_out, sums, sums_qkv, weight_fed, weight_in,
     a_parts, a_near, a_far, h_parts, h_near, h_far, stat_own, stat_got, stat_sum, stat_far,
     an_out, an_in, af_out, af_in, hn_out, hn_in, hf_out, hf_in, st_out, st_in, *row_scratch,
 ):
@@ -458,7 +462,8 @@
     going = []
 
     def meanwhile():
-        going.append(WeightGrads(here, feed0, feed1, feed2, feed3, row_scratch))
+        going.append(fed_grad(here, attended, grad_branch, row_scratch[:3]))
+        going.append(in_grad(here, hidden_two, grad_pre, row_scratch[3:]))
 
     grad_now = grad[...]
     grad_branch_now = (mod_own[:, 2:3] * grad_now).astype(BF16)
@@ -495,20 +500,21 @@
     sums[:, 2:3] = jnp.sum(grad_now * branch[...], 1, keepdims=True)
     sums[:, 3:4] = jnp.sum(grad_branch_now.astype(F32), 1, keepdims=True)
     sums_qkv[...] = jnp.sum(grad_qkv_now.astype(F32), 1, keepdims=True)
-    going[0].finish(weight_in, weight_fed)
+    weight_fed[...] = going[0].finish()
+    weight_in[...] = going[1].finish()
 
 
 def modulation_start(
-    sizes, signal, w_mod, b_mod, next_in, next_fed,
-    mod_all, signal_part, all_in, all_fed,
+    sizes, signal, w_mod, b_mod, next_in,
+    mod_all, signal_part, all_in,
     sig_row, sig_col, mod_part, mod_got, mod_col,
-    sig_row_sems, s_out, s_fwd, s_in, mod_sems, m_out, m_fwd, m_in, in_sems, fed_sems,
+    sig_row_sems, s_out, s_fwd, s_in, mod_sems, m_out, m_fwd, m_in, in_sems,
 ):
     here = Place(sizes)
     greet(here)
     width = signal.shape[1]
     signals = RowGather(here, signal, sig_row, sig_row_sems)
-    coming = [RowGather(here, next_in, all_in, in_sems), RowGather(here, next_fed, all_fed, fed_sems)]
+    coming = RowGather(here, next_in, all_in, in_sems)
     signals.finish()
     sig_col[here.col] = sig_row[...].reshape(here.rows * 8, width)
     gather(here, sig_col, s_out, s_fwd, s_in)
@@ -526,13 +532,12 @@
     mod_col[here.col] = total
     gather(here, mod_col, m_out, m_fwd, m_in)
     mod_all[...] = mod_col[...]
-    for one in coming:
-        one.finish()
+    coming.finish()
 
 
 def modulation_end(
-    sizes, grad_mod, biases, w_mod, feed0, feed1, feed2, feed3,
-    mod_all, bias_sum, grad_signal, weight_in, weight_fed,
+    sizes, grad_mod, biases, w_mod, hidden, grad_qkv,
+    mod_all, bias_sum, grad_signal, weight_in,
     mod_row, bias_row, back_col, back_own, back_row,
     mod_sems, bias_sems, b_out, b_fwd, b_in, back_sems, *row_scratch,
 ):
@@ -540,7 +545,7 @@
     greet(here)
     mods = RowGather(here, grad_mod, mod_row, mod_sems)
     shares = RowGather(here, biases, bias_row, bias_sems)
-    going = WeightGrads(here, feed0, feed1, feed2, feed3, row_scratch)
+    going = in_grad(here, hidden, grad_qkv, row_scratch)
     mods.finish()
     mod_all[...] = mod_row[...]
     product = 0.0
@@ -557,7 +562,7 @@
     grad_signal[...] = back_row[
         here.col // here.per_row, pl.ds(pl.multiple_of(here.row * 8, 8), 8)
     ]
-    going.finish(weight_in, weight_fed)
+    weight_in[...] = going.finish()
 
 
 def run(body, ident, args, outs, scratch, far_args=0, far_outs=0):
@@ -625,39 +630,30 @@
             )
         )
 
-    def gathered(first):
-        if first:
-            return [((rows, rows_in, 3 * width), BF16), ((rows, width, rows_in), BF16)]
-        return [((rows, rows_in, hidden_width), BF16), ((rows, width, rows_fed), BF16)]
-
-    def grads(first):
-        return [(shape[1:], F32) for shape, _ in gathered(first)]
-
-    def grad_scratch(first):
-        (one, _), (two, _) = gathered(first)
-        return [
-            pltpu.VMEM(one, BF16),
-            pltpu.VMEM(one, BF16),
-            pltpu.VMEM(two, BF16),
-            pltpu.VMEM(two, BF16),
-            dma(2, rows),
-            dma(2, rows),
-        ]
-
-    mod_all, signal_part, w_qkv, w_out = run(
+    shape_qkv = (rows, rows_in, 3 * width)
+    shape_out = (rows, width, rows_in)
+    shape_one = (rows, rows_in, hidden_width)
+    shape_two = (rows, width, rows_fed)
+
+    def sum_scratch(*shapes):
+        scratch = []
+        for shape in shapes:
+            scratch += [pltpu.VMEM(shape, BF16), pltpu.VMEM(shape, BF16), dma(2, rows)]
+        return scratch
+
+    mod_all, signal_part, w_qkv = run(
         functools.partial(modulation_start, sizes), 0,
         (
             jnp.broadcast_to(signal, (8, width)),
             w_mod_flat,
             b_mod.reshape(LAYERS, 1, 6 * width),
             shards[0][0],
-            shards[0][1],
         ),
         [
             ((count, LAYERS, 8, 6 * width), F32),
             ((per_row, rows * 8, width), F32),
-        ]
-        + gathered(True),
+            (shape_qkv, BF16),
+        ],
         [
             pltpu.VMEM((rows, 8, width), F32),
             pltpu.VMEM((count, rows * 8, width), F32),
@@ -666,9 +662,9 @@
             pltpu.VMEM((count, LAYERS, 8, 6 * width), F32),
             dma(2, rows), dma(count), dma(count), dma(count),
             dma(2, rows), dma(count), dma(count), dma(count),
-            dma(2, rows), dma(2, rows),
+            dma(2, rows),
         ],
-        2, 2,
+        1, 1,
     )
     mods = mod_all[:, :, 0].reshape(count, LAYERS, 6, width).transpose(1, 0, 3, 2)
     mod_full = mods.reshape(LAYERS, D, 6)
@@ -678,11 +674,11 @@
     saved = []
     for i in range(LAYERS):
         bias = jnp.concatenate([b_qv[i, 0], jnp.zeros_like(b_qv[i, 0]), b_qv[i, 1]])[:, None]
-        normed1, inverse1, hidden1, qkv, log_total, attended, branch1, stream, w_one, w_two = run(
+        normed1, inverse1, hidden1, qkv, log_total, attended, branch1, stream, w_out, w_one = run(
             functools.partial(attention_forward, sizes), 1,
             (
-                stream, mod_full[i], mod_own[i], w_qkv, bias, w_out,
-                attention_output_bias[i][:, None], shards[i][2], shards[i][3],
+                stream, mod_full[i], mod_own[i], w_qkv, bias,
+                attention_output_bias[i][:, None], shards[i][1], shards[i][2],
             ),
             [
                 ((D, length), F32),
@@ -693,19 +689,21 @@
                 ((rows, rows_in, length), BF16),
                 ((width, length), F32),
                 ((width, length), F32),
-            ]
-            + gathered(False),
-            gather_scratch(count, (width, width), length) + [dma(2, rows), dma(2, rows)],
-            2, 2,
+                (shape_out, BF16),
+                (shape_one, BF16),
+            ],
+            gather_scratch(count, (width, width), length)
+            + [pltpu.VMEM(shape_out, BF16), dma(2, rows), dma(2, rows)],
+            2, 1,
         )
         more = i + 1 < LAYERS
         results = run(
             functools.partial(mlp_forward, sizes, more), 2 if more else 3,
             (
-                stream, mod_full[i], mod_own[i], w_one, first_linear_bias[i][:, None], w_two,
-                second_linear_bias[i][:, None],
+                stream, mod_full[i], mod_own[i], w_one, first_linear_bias[i][:, None],
+                second_linear_bias[i][:, None], shards[i][3],
             )
-            + (shards[i + 1][:2] if more else ()),
+            + (shards[i + 1][:1] if more else ()),
             [
                 ((D, length), F32),
                 ((1, length), F32),
@@ -714,13 +712,15 @@
                 ((rows, rows_fed, length), BF16),
                 ((width, length), F32),
                 ((width, length), F32),
+                (shape_two, BF16),
             ]
-            + (gathered(True) if more else []),
+            + ([(shape_qkv, BF16)] if more else []),
             gather_scratch(count, (width, hidden_width), length)
-            + ([dma(2, rows), dma(2, rows)] if more else []),
-            2 if more else 0, 2 if more else 0,
-        )
-        normed2, inverse2, hidden2, pre, activated, branch2, stream = results[:7]
+            + [pltpu.VMEM(shape_two, BF16), dma(2, rows)]
+            + ([dma(2, rows)] if more else []),
+            2 if more else 1, 1 if more else 0,
+        )
+        normed2, inverse2, hidden2, pre, activated, branch2, stream, w_two = results[:8]
         saved.append(
             (
                 normed1, inverse1, hidden1, qkv, log_total, attended, branch1,
@@ -729,14 +729,16 @@
             )
         )
         if more:
-            w_qkv, w_out = results[7:]
+            w_qkv = results[8]
     output = stream.T.astype(BF16)
 
     grad = cotangent.astype(F32).T
     grad_mods = [None] * LAYERS
     biases = [None] * LAYERS
-    first_grads = [None] * LAYERS
-    second_grads = [None] * LAYERS
+    grads_qkv = [None] * LAYERS
+    grads_out = [None] * LAYERS
+    grads_one = [None] * LAYERS
+    grads_two = [None] * LAYERS
     waiting = None
     for i in reversed(range(LAYERS)):
         (
@@ -747,7 +749,7 @@
         more = waiting is not None
         results = run(
             functools.partial(mlp_backward, sizes, more), 6 if more else 4,
-            (grad, mod_full[i], mod_own[i], branch2, pre, normed2, inverse2, w_one, w_two)
+            (grad, mod_full[i], mod_own[i], branch2, pre, normed2, inverse2, w_one, w_two, activated)
             + (waiting if more else ()),
             [
                 ((width, length), BF16),
@@ -755,19 +757,20 @@
                 ((width, length), F32),
                 ((width, 4), F32),
                 ((hidden_width, 1), F32),
+                (shape_two[1:], F32),
             ]
-            + (grads(True) if more else []),
+            + ([(shape_qkv[1:], F32)] if more else []),
             scatter_scratch(count, (hidden_width, width), length)
-            + (grad_scratch(True) if more else []),
-        )
-        grad_branch2, grad_pre, grad, sums2, sums_pre = results[:5]
+            + sum_scratch(shape_two, *([shape_qkv] if more else [])),
+        )
+        grad_branch2, grad_pre, grad, sums2, sums_pre, grads_two[i] = results[:6]
         if more:
-            first_grads[i + 1] = results[5:]
-        grad_branch1, grad_qkv, grad, sums1, sums_qkv, *second_grads[i] = run(
+            grads_qkv[i + 1] = results[6]
+        grad_branch1, grad_qkv, grad, sums1, sums_qkv, grads_out[i], grads_one[i] = run(
             functools.partial(attention_backward, sizes), 5,
             (
                 grad, mod_full[i], mod_own[i], branch1, qkv, log_total, normed1, inverse1,
-                w_qkv, w_out, hidden2, grad_pre, activated, grad_branch2,
+                w_qkv, w_out, attended, hidden2, grad_pre,
             ),
             [
                 ((width, length), BF16),
@@ -775,18 +778,19 @@
                 ((width, length), F32),
                 ((width, 4), F32),
                 ((3 * width, 1), F32),
-            ]
-            + grads(False),
-            scatter_scratch(count, (width, width), length) + grad_scratch(False),
-        )
-        waiting = (hidden1, grad_qkv, attended, grad_branch1)
+                (shape_out[1:], F32),
+                (shape_one[1:], F32),
+            ],
+            scatter_scratch(count, (width, width), length) + sum_scratch(shape_out, shape_one),
+        )
+        waiting = (hidden1, grad_qkv)
         grad_mods[i] = jnp.concatenate([sums1[:, 0:3], sums2[:, 0:3]], axis=1).T.astype(BF16)
         biases[i] = jnp.concatenate(
             [sums_qkv[:width, 0], sums_qkv[2 * width :, 0], sums1[:, 3], sums2[:, 3], sums_pre[:, 0]]
         )
     mod_grad = jnp.stack(grad_mods).reshape(LAYERS, 1, 6 * width).astype(F32)
     bias_grad = jnp.stack(biases).reshape(1, -1)
-    mod_grad_all, bias_sum, grad_signal, *first_grads[0] = run(
+    mod_grad_all, bias_sum, grad_signal, grads_qkv[0] = run(
         functools.partial(modulation_end, sizes), 7,
         (
             jnp.broadcast_to(mod_grad, (LAYERS, 8, 6 * width)),
@@ -798,8 +802,8 @@
             ((rows, LAYERS, 8, 6 * width), F32),
             ((8, bias_grad.shape[1]), F32),
             ((8, rows_in), F32),
-        ]
-        + grads(True),
+            (shape_qkv[1:], F32),
+        ],
         [
             pltpu.VMEM((rows, LAYERS, 8, 6 * width), F32),
             pltpu.VMEM((rows, 8, bias_grad.shape[1]), F32),
@@ -808,18 +812,16 @@
             pltpu.VMEM((rows, rows * 8, rows_in), F32),
             dma(2, rows), dma(2, rows), dma(count), dma(count), dma(count), dma(2, rows),
         ]
-        + grad_scratch(True),
+        + sum_scratch(shape_qkv),
     )
     signals = signal_part.reshape(per_row, rows, 8, width)[:, :, 0]
     signals = signals.transpose(1, 0, 2).reshape(rows, rows_in)
     mod_rows = mod_grad_all[:, :, 0]
-    grad_w_mod = jnp.einsum(
-        "ri,rlj->lij",
-        signals.astype(BF16),
-        mod_rows.astype(BF16),
-        preferred_element_type=F32,
-    ).reshape(LAYERS, rows_in, 6, width)
-    grad_b_mod = jnp.sum(mod_rows, 0).reshape(LAYERS, 6, width)
+    mod_rows = mod_rows.reshape(rows, LAYERS, 6, width)
+    grad_w_mod = sum(
+        signals[r][None, :, None, None] * mod_rows[r][:, None] for r in range(rows)
+    )
+    grad_b_mod = jnp.sum(mod_rows, 0)
     grad_signal = lax.dynamic_slice(
         grad_signal[:1], (0, lax.axis_index("col") % per_row * width), (1, width)
     )
@@ -831,13 +833,13 @@
         grad_cond,
         grad_w_mod,
         grad_b_mod,
-        jnp.stack([one[0] for one in first_grads]).reshape(LAYERS, rows_in, 3, width),
+        jnp.stack(grads_qkv).reshape(LAYERS, rows_in, 3, width),
         bias_sum[:, : 2 * width].reshape(LAYERS, 2, width),
-        jnp.stack([one[1].T for one in first_grads]),
+        jnp.stack([one.T for one in grads_out]),
         bias_sum[:, 2 * width : 3 * width],
-        jnp.stack([one[0] for one in second_grads]),
+        jnp.stack(grads_one),
         bias_sum[:, 4 * width :],
-        jnp.stack([one[1].T for one in second_grads]),
+        jnp.stack([one.T for one in grads_two]),
         bias_sum[:, 3 * width : 4 * width],
     )
 

time: 440 us -> 390 us (0.89)
  Pallas kernels: 409 us -> 362 us
    pallas_call x10, Pallas kernels: 409 us -> 362 us  [run(): pl.pallas_call(body, out_shape=[jax.ShapeDtypeStruct(shape, dtype) for sh...]
where the time goes in v3:
time: 390 us
  Pallas kernels  362 us (93%)
  local copies, waits for them, and re-layouts  15.6 us (4%)
  other arithmetic  10.4 us (3%)
    pallas_call x10, Pallas kernels, run(): pl.pallas_call(body, out_shape=[jax.ShapeDtypeStruct(shape, dtype) for sh...  362 us

profile of v3, /device:TPU:0, one launch (start us, length us, event | category | flops | bytes accessed | tf_op | source)
XLA Modules:
  0.0 389.9 jit_solution(578554654894963907)
XLA Ops:
  0.7 1.0 convert_bitcast_fusion.1.stream
  1.6 0.7 convert_convert_fusion
  2.3 1.7 copy.56.w_mod
  4.5 29.6 %shard_map.228 = (f32[8,2,8,864]{3,2,1,0:T(8,128)S(1)}, f32[2,32,144]{2,1,0:T(8,128)S(1)}, bf16[4,288,432]{2,1,0:T(8,128)(2,1)}) custom-call(f32[8,144]{1,0:T(8,128)S(1)} %broadcast_in_dim.30.signal, bf16[2,288,864]{2,1,0:T(8,128)(2,1)S(1)} %copy.56.w_mod, f32[2,1,864]{2,1,0:T(1,128)S(1)} %reshape.109.b_mod, bf16[288,432]{1,0:T(8,128)(2,1)S(1)} %copy.58.next_in), custom_call_target="tpu_custom_call" | custom-call | tf_op jit(solution)/shard_map/pallas_call | solution.py:571
  34.2 1.1 copy.60
  36.0 30.2 %shard_map.229 = (f32[1152,256]{1,0:T(8,128)}, f32[1,256]{1,0:T(1,128)S(1)}, bf16[1152,256]{1,0:T(8,128)(2,1)}, bf16[6,72,256]{2,1,0:T(8,128)(2,1)S(1)}, f32[2,1...) custom-call(f32[144,256]{1,0:T(8,128)S(1)} %convert_bitcast_fusion.1, ...), custom_call_target="tpu_custom_call" | custom-call | tf_op jit(solution)/shard_map/pallas_call | solution.py:571
  66.2 0.8 copy-done.4
  67.3 1.1 slice_bitcast_fusion.2
  68.6 40.5 %shard_map.230 = (f32[1152,256]{1,0:T(8,128)}, f32[1,256]{1,0:T(1,128)S(1)}, bf16[1152,256]{1,0:T(8,128)(2,1)}, f32[576,256]{1,0:T(8,128)}, bf16[4,1152,256]{2,1...) custom-call(f32[144,256]{1,0:T(8,128)S(1)} %get-tuple-element.82.ref, ...), custom_call_target="tpu_custom_call" | custom-call | tf_op jit(solution)/shard_map/pallas_call | solution.py:571
  109.2 1.1 copy.67
  110.5 34.8 %shard_map.231 = (f32[1152,256]{1,0:T(8,128)}, f32[1,256]{1,0:T(1,128)S(1)}, bf16[1152,256]{1,0:T(8,128)(2,1)}, bf16[6,72,256]{2,1,0:T(8,128)(2,1)S(1)}, f32[2,1...) custom-call(f32[144,256]{1,0:T(8,128)S(1)} %get-tuple-element.84.str, ...), custom_call_target="tpu_custom_call" | custom-call | tf_op jit(solution)/shard_map/pallas_call | solution.py:571
  145.3 0.8 copy-done.5
  146.3 39.6 %shard_map.232 = (f32[1152,256]{1,0:T(8,128)}, f32[1,256]{1,0:T(1,128)S(1)}, bf16[1152,256]{1,0:T(8,128)(2,1)S(1)}, f32[576,256]{1,0:T(8,128)}, bf16[4,1152,256]...) custom-call(f32[144,256]{1,0:T(8,128)S(1)} %get-tuple-element.86.refs_0_, ...), custom_call_target="tpu_custom_call" | custom-call | tf_op jit(solution)/shard_map/pallas_call | solution.py:571
  186.0 0.8 copy-done.3
  186.8 0.6 convert_bitcast_fusion.2
  187.4 52.4 %shard_map.233 = (bf16[144,256]{1,0:T(8,128)(2,1)}, bf16[576,256]{1,0:T(8,128)(2,1)S(1)}, f32[144,256]{1,0:T(8,128)S(1)}, f32[144,4]{1,0:T(8,128)S(1)}, f32[576,1]{1,0:T(8,128)S(1)}, /*index=5*/f32[144,1152]{1,0:T(8,128)}) custom-call(f32[144,256]{1,0:T(8,128)S(1)} %convert_bitcast_fusion.refs_0_, f32[1152,6]{1,0:T(8,128)S(1)} %bitcast.90, ...), custom_call_target="tpu_custom_call" | custom-call | tf_op jit(solution)/shard_map/pallas_call | solution.py:571
  239.8 31.5 %shard_map.234 = (bf16[144,256]{1,0:T(8,128)(2,1)}, bf16[432,256]{1,0:T(8,128)(2,1)S(1)}, f32[144,256]{1,0:T(8,128)S(1)}, f32[144,4]{1,0:T(8,128)S(1)}, f32[432,...) custom-call(f32[144,256]{1,0:T(8,128)S(1)} %get-tuple-element.95.grad, f32[1152,6]{1,0:T(8,128)} %bitcast.89, ...), custom_call_target="tpu_custom_call" | custom-call | tf_op jit(solution)/shard_map/pallas_call | solution.py:571
  271.3 46.3 %shard_map.235 = (bf16[144,256]{1,0:T(8,128)(2,1)}, bf16[576,256]{1,0:T(8,128)(2,1)S(1)}, f32[144,256]{1,0:T(8,128)S(1)}, f32[144,4]{1,0:T(8,128)S(1)}, f32[576,...) custom-call(f32[144,256]{1,0:T(8,128)S(1)} %get-tuple-element.105.refs_0_, f32[1152,6]{1,0:T(8,128)} %bitcast.97, ...), custom_call_target="tpu_custom_call" | custom-call | tf_op jit(solution)/shard_map/pallas_call | solution.py:571
  317.7 30.9 %shard_map.236 = (bf16[144,256]{1,0:T(8,128)(2,1)}, bf16[432,256]{1,0:T(8,128)(2,1)S(1)}, f32[144,256]{1,0:T(8,128)S(1)}, f32[144,4]{1,0:T(8,128)S(1)}, f32[432,...) custom-call(f32[144,256]{1,0:T(8,128)S(1)} %get-tuple-element.114.grad, f32[1152,6]{1,0:T(8,128)} %bitcast.98, ...), custom_call_target="tpu_custom_call" | custom-call | tf_op jit(solution)/shard_map/pallas_call | solution.py:571
  350.8 26.7 %shard_map.237 = (f32[4,2,8,864]{3,2,1,0:T(8,128)S(1)}, f32[8,2304]{1,0:T(8,128)S(1)}, f32[8,288]{1,0:T(8,128)S(1)}, f32[288,432]{1,0:T(8,128)S(1)}) custom-call(f32[2,8,864]{2,1,0:T(8,128)S(1)} %broadcast_in_dim.33.grad_mod, f32[8,2304]{1,0:T(8,128)S(1)} %broadcast_in_dim.35.biases, bf16[2,288,864]{2,1,0:T(8,128)(2,1)} %copy-done.1, ...), custom_call_target="tpu_custom_call" | custom-call | tf_op jit(solution)/shard_map/pallas_call | solution.py:571
  377.5 0.6 fusion.3
  379.0 2.6 multiply_add_fusion
  381.7 0.6 copy.79
  382.5 0.2 copy.77
  382.8 1.2 pad_maximum_fusion.1
  384.1 0.7 reshape.107
  384.7 0.8 pad_maximum_fusion.3
  385.5 0.7 fusion.6
  386.2 1.2 pad_maximum_fusion
  387.4 0.7 slice.251
  388.1 1.2 pad_maximum_fusion.2
  389.2 0.7 copy.89
  (115 shorter events, 5.3 us)
Async XLA Ops:
  0.6 3.4 copy-start.15
  0.7 3.5 copy-start.9
  4.0 30.0 %copy-start.1 = (bf16[2,288,864]{2,1,0:T(8,128)(2,1)}, bf16[2,288,864]{2,1,0:T(8,128)(2,1)S(1)}, u32[]{:S(2)}) copy-start(bf16[2,288,864]{2,1,0:T(8,128)(2,1)S(1)} %copy.56.w_mod) | copy-start | bytes 2985988
  4.4 31.1 %copy-start.17 = (f32[2,2,144]{2,1,0:T(2,128)S(1)}, f32[2,2,144]{2,1,0:T(2,128)}, u32[]{:S(2)}) copy-start(f32[2,2,144]{2,1,0:T(2,128)} %param.18) | copy-start | bytes 6916
  4.4 31.3 %copy-start.19 = (f32[2,144]{1,0:T(2,128)S(1)}, f32[2,144]{1,0:T(2,128)}, u32[]{:S(2)}) copy-start(f32[2,144]{1,0:T(2,128)} %param.20) | copy-start | bytes 3460
  4.4 31.4 %copy-start.13 = (bf16[2,288,144]{1,2,0:T(8,128)(2,1)S(1)}, bf16[2,288,144]{1,2,0:T(8,128)(2,1)}, u32[]{:S(2)}) copy-start(bf16[2,288,144]{1,2,0:T(8,128)(2,1)} %param.19) | copy-start | bytes 497668
  34.0 1.9 copy-start.6
  36.0 31.0 %copy-start.16 = (f32[2,576]{1,0:T(2,128)S(1)}, f32[2,576]{1,0:T(2,128)}, u32[]{:S(2)}) copy-start(f32[2,576]{1,0:T(2,128)} %param.22) | copy-start | bytes 13828
  36.0 31.1 %copy-start.20 = (f32[2,144]{1,0:T(2,128)S(1)}, f32[2,144]{1,0:T(2,128)}, u32[]{:S(2)}) copy-start(f32[2,144]{1,0:T(2,128)} %param.24) | copy-start | bytes 3460
  66.2 0.8 copy-start.4
  145.3 0.8 copy-start.5
  146.3 41.1 %copy-start.14 = (bf16[256,144]{0,1:T(8,128)(2,1)S(1)}, bf16[256,144]{0,1:T(8,128)(2,1)}, u32[]{:S(2)}) copy-start(bf16[256,144]{0,1:T(8,128)(2,1)} %param.25) | copy-start | bytes 221188
  146.3 41.1 %copy-start = (f32[1,8,144,6]{3,2,1,0:T(8,128)S(1)}, f32[1,8,144,6]{3,2,1,0:T(8,128)}, u32[]{:S(2)}) copy-start(f32[1,8,144,6]{3,2,1,0:T(8,128)} %copy.67) | copy-start | bytes 82948
  185.9 0.8 copy-start.3
  348.6 2.2 copy-start.2
  349.9 27.6 %copy-start.18 = (bf16[1,144]{1,0:T(2,128)(2,1)S(1)}, bf16[1,144]{1,0:T(2,128)(2,1)}, u32[]{:S(2)}) copy-start(bf16[1,144]{1,0:T(2,128)(2,1)} %param.14) | copy-start | bytes 868
  378.3 4.0 %copy-start.12 = (f32[288,432]{1,0:T(8,128)S(1)}, f32[288,432]{1,0:T(8,128)}, u32[]{:S(2)}) copy-start(f32[288,432]{1,0:T(8,128)} %get-tuple-element.139) | copy-start | bytes 1492996
  382.8 3.4 copy-start.8
  384.0 2.2 copy-start.7
  386.2 1.9 copy-start.10
  386.2 1.9 copy-start.11

commit v4 on v3

--- a/solution.py
+++ b/solution.py
@@ -198,6 +198,104 @@
     for r in range(here.rows):
         parts[r] = nt(grad_now, fed[r]).astype(BF16)
     return RowSum(here, parts, got, sems)
+
+
+def gather_chain(here, buf, out_sem, fwd_sem, in_sem):
+    z, zs, core = here.z, here.zs, here.core
+    above, below = here.peer(here.ahead(1)), here.peer(here.behind(1))
+
+    def go(src, device, sem):
+        return send(buf.at[src], buf.at[src], sem, in_sem.at[src], device)
+
+    own = here.col
+    pl.when(z < zs - 1)(lambda: go(own, above, out_sem.at[0]).start())
+    pl.when(z > 0)(lambda: go(own, below, out_sem.at[zs]).start())
+    go(own, here.mate, fwd_sem.at[z]).start()
+
+    def pass_on(src_z, further, device, sem):
+        src = src_z * 2 + core
+        go(src, device, sem).wait_recv()
+        pl.when(further)(lambda: go(src, device, sem).start())
+        go(src, here.mate, fwd_sem.at[src_z]).start()
+
+    for k in range(1, zs):
+        pl.when(z >= k)(
+            functools.partial(pass_on, here.behind(k), z < zs - 1, above, out_sem.at[k])
+        )
+        pl.when(z + k < zs)(
+            functools.partial(pass_on, here.ahead(k), z > 0, below, out_sem.at[zs + k])
+        )
+    for k in range(zs):
+        src = here.behind(k) * 2 + here.mate_core
+        go(src, here.mate, fwd_sem.at[here.behind(k)]).wait_recv()
+    for k in range(zs):
+        go(own, here.mate, fwd_sem.at[k]).wait_send()
+        pl.when((z >= k) & (z < zs - 1))(lambda: go(own, above, out_sem.at[k]).wait_send())
+        pl.when((z + k < zs) & (z > 0))(lambda: go(own, below, out_sem.at[zs + k]).wait_send())
+
+
+def scatter_chain(here, parts, near, up, down, near_sems, up_sems, down_sems, meanwhile):
+    near_out, near_in = near_sems
+    z, zs, core = here.z, here.zs, here.core
+    above, below = here.peer(here.ahead(1)), here.peer(here.behind(1))
+
+    def swap(d):
+        return send(
+            parts.at[here.mate_core, d], near.at[d], near_out.at[d], near_in.at[d], here.mate
+        )
+
+    def hop(d, buf, sems, device):
+        return send(parts.at[core, d], buf.at[d], sems[0].at[d], sems[1].at[d], device)
+
+    order = []
+    for i in range(zs - 1):
+        order += [(zs - 1 - i, True), (i, False)]
+    sent = []
+    for d, _ in order:
+        if d not in sent:
+            sent.append(d)
+            swap(d).start()
+
+    @pl.when(z == 0)
+    def _():
+        up[0] = jnp.zeros(up.shape[1:], BF16)
+
+    @pl.when(z == zs - 1)
+    def _():
+        down[zs - 1] = jnp.zeros(down.shape[1:], BF16)
+
+    def one(d, buf, sems, device, first):
+        swap(d).wait_recv()
+        both = parts[core, d].astype(F32) + near[d].astype(F32)
+
+        @pl.when(first)
+        def _():
+            parts[core, d] = both.astype(BF16)
+
+        @pl.when(jnp.logical_not(first))
+        def _():
+            hop(d, buf, sems, device).wait_recv()
+            parts[core, d] = (both + buf[d].astype(F32)).astype(BF16)
+
+        hop(d, buf, sems, device).start()
+
+    for i, (d, upward) in enumerate(order):
+        if upward:
+            pl.when(z < d)(functools.partial(one, d, up, up_sems, above, z == 0))
+        else:
+            pl.when(z > d)(functools.partial(one, d, down, down_sems, below, z == zs - 1))
+        if i == 1:
+            meanwhile()
+    swap(z).wait_recv()
+    total = parts[core, z].astype(F32) + near[z].astype(F32)
+    pl.when(z > 0)(lambda: hop(z, up, up_sems, above).wait_recv())
+    pl.when(z < zs - 1)(lambda: hop(z, down, down_sems, below).wait_recv())
+    total = total + up[z].astype(F32) + down[z].astype(F32)
+    for d in range(zs):
+        swap(d).wait_send()
+        pl.when(z < d)(lambda: hop(d, up, up_sems, above).wait_send())
+        pl.when(z > d)(lambda: hop(d, down, down_sems, below).wait_send())
+    return total
 
 
 def scatter_sum(here, parts, near, far, near_sems, far_sems, stat=None, meanwhile=None):
@@ -360,7 +458,7 @@
     pre_now = tn(flat(w_one[...]), hidden_now) + b_one[...]
     pre[...] = pre_now
     a_buf[here.col] = gelu(pre_now).astype(BF16)
-    gather(here, a_buf, a_out, a_fwd, a_in)
+    gather_chain(here, a_buf, a_out, a_fwd, a_in)
     needed.finish()
     w_two[...] = w_buf[...]
     branch_now = b_two[...] + fed_product(here, w_buf, a_buf, activated)
@@ -413,21 +511,23 @@
         refs = refs[1:]
     a_parts, a_near, a_far, h_parts, h_near, h_far, stat_own, stat_got, stat_sum, stat_far = refs[:10]
     an_out, an_in, af_out, af_in, hn_out, hn_in, hf_out, hf_in, st_out, st_in = refs[10:20]
+    a_down, ad_out, ad_in = refs[20:23]
     here = Place(sizes)
     greet(here)
     going = []
 
     def meanwhile():
-        going.append(fed_grad(here, activated, grad_branch, refs[20:23]))
+        going.append(fed_grad(here, activated, grad_branch, refs[23:26]))
         if more:
-            going.append(in_grad(here, *feeds, refs[23:26]))
+            going.append(in_grad(here, *feeds, refs[26:29]))
 
     grad_now = grad[...]
     grad_branch_now = (mod_own[:, 5:6] * grad_now).astype(BF16)
     grad_branch[...] = grad_branch_now
     split_parts(here, a_parts, w_two, grad_branch_now)
-    grad_act, _ = scatter_sum(
-        here, a_parts, a_near, a_far, (an_out, an_in), (af_out, af_in), None, meanwhile
+    grad_act = scatter_chain(
+        here, a_parts, a_near, a_far, a_down,
+        (an_out, an_in), (af_out, af_in), (ad_out, ad_in), meanwhile,
     )
     grad_pre_now = (grad_act * gelu_slope(pre[...])).astype(BF16)
     grad_pre[...] = grad_pre_now
@@ -761,6 +861,8 @@
             ]
             + ([(shape_qkv[1:], F32)] if more else []),
             scatter_scratch(count, (hidden_width, width), length)
+            + [pltpu.VMEM((count // 2, hidden_width, length), BF16)]
+            + [dma(count // 2), dma(count // 2)]
             + sum_scratch(shape_two, *([shape_qkv] if more else [])),
         )
         grad_branch2, grad_pre, grad, sums2, sums_pre, grads_two[i] = results[:6]

time: 390 us -> 406 us (1.041)
  Pallas kernels: 362 us -> 379 us
    pallas_call x10, Pallas kernels: 362 us -> 379 us  [run(): pl.pallas_call(body, out_shape=[jax.ShapeDtypeStruct(shape, dtype) for sh...]
where the time goes in v4:
time: 406 us
  Pallas kernels  379 us (93%)
  local copies, waits for them, and re-layouts  15.6 us (4%)
  other arithmetic  10.4 us (3%)
    pallas_call x10, Pallas kernels, run(): pl.pallas_call(body, out_shape=[jax.ShapeDtypeStruct(shape, dtype) for sh...  379 us

profile of v4, /device:TPU:0, one launch (start us, length us, event | category | flops | bytes accessed | tf_op | source)
XLA Modules:
  0.0 406.0 jit_solution(4833023657349234578)
XLA Ops:
  0.7 1.0 convert_bitcast_fusion.1.stream
  1.6 0.7 convert_convert_fusion
  2.3 1.7 copy.56.w_mod
  4.5 29.6 %shard_map.228 = (f32[8,2,8,864]{3,2,1,0:T(8,128)S(1)}, f32[2,32,144]{2,1,0:T(8,128)S(1)}, bf16[4,288,432]{2,1,0:T(8,128)(2,1)}) custom-call(f32[8,144]{1,0:T(8,128)S(1)} %broadcast_in_dim.30.signal, bf16[2,288,864]{2,1,0:T(8,128)(2,1)S(1)} %copy.56.w_mod, f32[2,1,864]{2,1,0:T(1,128)S(1)} %reshape.109.b_mod, bf16[288,432]{1,0:T(8,128)(2,1)S(1)} %copy.58.next_in), custom_call_target="tpu_custom_call" | custom-call | tf_op jit(solution)/shard_map/pallas_call | solution.py:671
  34.2 1.1 copy.60
  36.0 30.2 %shard_map.229 = (f32[1152,256]{1,0:T(8,128)}, f32[1,256]{1,0:T(1,128)S(1)}, bf16[1152,256]{1,0:T(8,128)(2,1)}, bf16[6,72,256]{2,1,0:T(8,128)(2,1)S(1)}, f32[2,1...) custom-call(f32[144,256]{1,0:T(8,128)S(1)} %convert_bitcast_fusion.1, ...), custom_call_target="tpu_custom_call" | custom-call | tf_op jit(solution)/shard_map/pallas_call | solution.py:671
  66.2 0.8 copy-done.4
  67.3 1.1 slice_bitcast_fusion.2
  68.6 43.5 %shard_map.230 = (f32[1152,256]{1,0:T(8,128)}, f32[1,256]{1,0:T(1,128)S(1)}, bf16[1152,256]{1,0:T(8,128)(2,1)}, f32[576,256]{1,0:T(8,128)}, bf16[4,1152,256]{2,1...) custom-call(f32[144,256]{1,0:T(8,128)S(1)} %get-tuple-element.82.ref, ...), custom_call_target="tpu_custom_call" | custom-call | tf_op jit(solution)/shard_map/pallas_call | solution.py:671
  112.2 1.1 copy.67
  113.5 27.8 %shard_map.231 = (f32[1152,256]{1,0:T(8,128)}, f32[1,256]{1,0:T(1,128)S(1)}, bf16[1152,256]{1,0:T(8,128)(2,1)}, bf16[6,72,256]{2,1,0:T(8,128)(2,1)S(1)}, f32[2,1...) custom-call(f32[144,256]{1,0:T(8,128)S(1)} %get-tuple-element.84.str, ...), custom_call_target="tpu_custom_call" | custom-call | tf_op jit(solution)/shard_map/pallas_call | solution.py:671
  141.3 0.8 copy-done.5
  142.4 42.7 %shard_map.232 = (f32[1152,256]{1,0:T(8,128)}, f32[1,256]{1,0:T(1,128)S(1)}, bf16[1152,256]{1,0:T(8,128)(2,1)S(1)}, f32[576,256]{1,0:T(8,128)}, bf16[4,1152,256]...) custom-call(f32[144,256]{1,0:T(8,128)S(1)} %get-tuple-element.86.refs_0_, ...), custom_call_target="tpu_custom_call" | custom-call | tf_op jit(solution)/shard_map/pallas_call | solution.py:671
  185.1 0.8 copy-done.3
  185.9 0.6 convert_bitcast_fusion.2
  186.6 51.1 %shard_map.233 = (bf16[144,256]{1,0:T(8,128)(2,1)}, bf16[576,256]{1,0:T(8,128)(2,1)S(1)}, f32[144,256]{1,0:T(8,128)S(1)}, f32[144,4]{1,0:T(8,128)S(1)}, f32[576,1]{1,0:T(8,128)S(1)}, /*index=5*/f32[144,1152]{1,0:T(8,128)}) custom-call(f32[144,256]{1,0:T(8,128)S(1)} %convert_bitcast_fusion.refs_0_, f32[1152,6]{1,0:T(8,128)S(1)} %bitcast.90, ...), custom_call_target="tpu_custom_call" | custom-call | tf_op jit(solution)/shard_map/pallas_call | solution.py:671
  237.7 34.7 %shard_map.234 = (bf16[144,256]{1,0:T(8,128)(2,1)}, bf16[432,256]{1,0:T(8,128)(2,1)S(1)}, f32[144,256]{1,0:T(8,128)S(1)}, f32[144,4]{1,0:T(8,128)S(1)}, f32[432,...) custom-call(f32[144,256]{1,0:T(8,128)S(1)} %get-tuple-element.95.grad, f32[1152,6]{1,0:T(8,128)} %bitcast.89, ...), custom_call_target="tpu_custom_call" | custom-call | tf_op jit(solution)/shard_map/pallas_call | solution.py:671
  272.4 52.4 %shard_map.235 = (bf16[144,256]{1,0:T(8,128)(2,1)}, bf16[576,256]{1,0:T(8,128)(2,1)S(1)}, f32[144,256]{1,0:T(8,128)S(1)}, f32[144,4]{1,0:T(8,128)S(1)}, f32[576,...) custom-call(f32[144,256]{1,0:T(8,128)S(1)} %get-tuple-element.105.refs_0_, f32[1152,6]{1,0:T(8,128)} %bitcast.97, ...), custom_call_target="tpu_custom_call" | custom-call | tf_op jit(solution)/shard_map/pallas_call | solution.py:671
  324.9 39.5 %shard_map.236 = (bf16[144,256]{1,0:T(8,128)(2,1)}, bf16[432,256]{1,0:T(8,128)(2,1)S(1)}, f32[144,256]{1,0:T(8,128)S(1)}, f32[144,4]{1,0:T(8,128)S(1)}, f32[432,...) custom-call(f32[144,256]{1,0:T(8,128)S(1)} %get-tuple-element.114.grad, f32[1152,6]{1,0:T(8,128)} %bitcast.98, ...), custom_call_target="tpu_custom_call" | custom-call | tf_op jit(solution)/shard_map/pallas_call | solution.py:671
  366.5 27.1 %shard_map.237 = (f32[4,2,8,864]{3,2,1,0:T(8,128)S(1)}, f32[8,2304]{1,0:T(8,128)S(1)}, f32[8,288]{1,0:T(8,128)S(1)}, f32[288,432]{1,0:T(8,128)S(1)}) custom-call(f32[2,8,864]{2,1,0:T(8,128)S(1)} %broadcast_in_dim.33.grad_mod, f32[8,2304]{1,0:T(8,128)S(1)} %broadcast_in_dim.35.biases, bf16[2,288,864]{2,1,0:T(8,128)(2,1)} %copy-done.1, ...), custom_call_target="tpu_custom_call" | custom-call | tf_op jit(solution)/shard_map/pallas_call | solution.py:671
  393.6 0.6 fusion.3
  395.1 2.6 multiply_add_fusion
  397.8 0.6 copy.79
  398.7 0.2 copy.77
  398.9 1.2 pad_maximum_fusion.1
  400.2 0.7 reshape.107
  400.9 0.8 pad_maximum_fusion.3
  401.7 0.7 fusion.6
  402.3 1.2 pad_maximum_fusion
  403.5 0.7 slice.251
  404.2 1.2 pad_maximum_fusion.2
  405.4 0.7 copy.89
  (115 shorter events, 5.3 us)
Async XLA Ops:
  0.6 3.4 copy-start.15
  0.7 3.5 copy-start.9
  4.0 30.0 %copy-start.1 = (bf16[2,288,864]{2,1,0:T(8,128)(2,1)}, bf16[2,288,864]{2,1,0:T(8,128)(2,1)S(1)}, u32[]{:S(2)}) copy-start(bf16[2,288,864]{2,1,0:T(8,128)(2,1)S(1)} %copy.56.w_mod) | copy-start | bytes 2985988
  4.4 31.1 %copy-start.17 = (f32[2,2,144]{2,1,0:T(2,128)S(1)}, f32[2,2,144]{2,1,0:T(2,128)}, u32[]{:S(2)}) copy-start(f32[2,2,144]{2,1,0:T(2,128)} %param.18) | copy-start | bytes 6916
  4.4 31.3 %copy-start.19 = (f32[2,144]{1,0:T(2,128)S(1)}, f32[2,144]{1,0:T(2,128)}, u32[]{:S(2)}) copy-start(f32[2,144]{1,0:T(2,128)} %param.20) | copy-start | bytes 3460
  4.4 31.4 %copy-start.13 = (bf16[2,288,144]{1,2,0:T(8,128)(2,1)S(1)}, bf16[2,288,144]{1,2,0:T(8,128)(2,1)}, u32[]{:S(2)}) copy-start(bf16[2,288,144]{1,2,0:T(8,128)(2,1)} %param.19) | copy-start | bytes 497668
  34.0 1.9 copy-start.6
  36.0 31.0 %copy-start.16 = (f32[2,576]{1,0:T(2,128)S(1)}, f32[2,576]{1,0:T(2,128)}, u32[]{:S(2)}) copy-start(f32[2,576]{1,0:T(2,128)} %param.22) | copy-start | bytes 13828
  36.0 31.1 %copy-start.20 = (f32[2,144]{1,0:T(2,128)S(1)}, f32[2,144]{1,0:T(2,128)}, u32[]{:S(2)}) copy-start(f32[2,144]{1,0:T(2,128)} %param.24) | copy-start | bytes 3460
  66.2 0.8 copy-start.4
  141.3 0.8 copy-start.5
  142.4 44.2 %copy-start.14 = (bf16[256,144]{0,1:T(8,128)(2,1)S(1)}, bf16[256,144]{0,1:T(8,128)(2,1)}, u32[]{:S(2)}) copy-start(bf16[256,144]{0,1:T(8,128)(2,1)} %param.25) | copy-start | bytes 221188
  142.4 44.2 %copy-start = (f32[1,8,144,6]{3,2,1,0:T(8,128)S(1)}, f32[1,8,144,6]{3,2,1,0:T(8,128)}, u32[]{:S(2)}) copy-start(f32[1,8,144,6]{3,2,1,0:T(8,128)} %copy.67) | copy-start | bytes 82948
  185.1 0.8 copy-start.3
  364.3 2.2 copy-start.2
  365.7 28.0 %copy-start.18 = (bf16[1,144]{1,0:T(2,128)(2,1)S(1)}, bf16[1,144]{1,0:T(2,128)(2,1)}, u32[]{:S(2)}) copy-start(bf16[1,144]{1,0:T(2,128)(2,1)} %param.14) | copy-start | bytes 868
  394.5 4.0 copy-start.12
  398.9 3.4 copy-start.8
  400.1 2.2 copy-start.7
  402.3 1.9 copy-start.10
  402.3 1.9 copy-start.11
